TPU v7x, 128 devices: a whole 4x4x4 slice. The times are simulated.
128 devices in a mesh: px: 8 (over y_hi, x), py: 16 (over z, y_lo, core).
Axes of the slice: x: 4, y: 4 (y_hi: 2, y_lo: 2; y = y_hi * 2 + y_lo), z: 4, core: 2. Of those that a mesh axis runs over, the one named last changes fastest.
Arguments:
- out_grad: float32 [4, 32, 128, 128, 128], P(None, None, 'px', 'py'), may hold values from -6 to 6
- input_modes: bfloat16 [4, 32, 64, 64, 66], P(None, None, 'px', 'py'), may hold values from -6 to 6
- mode_weights: bfloat16 [32, 32, 64, 64, 66], P(None, None, 'px', 'py'), may hold values from -1 to 1
Outputs:
- weight_grad: bfloat16 [32, 32, 64, 64, 66], P(None, None, 'px', 'py')
- input_grad: bfloat16 [4, 32, 128, 128, 128], P(None, None, 'px', 'py')
All inputs are finite; a program needn't handle non-finite values.
Results may differ from a plain program's by a relative error of at most 0.0057.
Values may be sent and summed in bfloat16 or wider, within the bound.
A program may use at most 192 MiB of HBM per device.

v0:
```python
import math

import jax
import jax.numpy as jnp
from jax import lax
from jax.sharding import PartitionSpec as P

KXM = 64
KYM = 64
KZM = 33


HIGH = lax.Precision.HIGHEST


def kept_wavenumbers(kept, length):
    counter = jnp.arange(kept, dtype=jnp.int32)
    return jnp.where(counter < kept // 2, counter, counter + (length - kept))


def twiddle_tables(wavenumbers, length):
    position = jnp.arange(length, dtype=jnp.int32)
    turn_count = wavenumbers[:, None] * position[None, :] % length
    phase_angle = turn_count.astype(jnp.float32) * jnp.float32(2.0 * math.pi / length)
    norm_factor = jnp.float32(1.0 / math.sqrt(length))
    return (jnp.cos(phase_angle) * norm_factor, jnp.sin(phase_angle) * norm_factor)


def z_tables(kept, length):
    cosine, sine = twiddle_tables(jnp.arange(kept, dtype=jnp.int32), length)
    forward_z = jnp.concatenate([cosine.T, -sine.T], axis=1)
    weighting = jnp.where(jnp.arange(kept) == 0, 1.0, 2.0).astype(jnp.float32)
    inverse_z = jnp.concatenate([weighting[:, None] * cosine, -weighting[:, None] * sine], axis=0)
    return (forward_z, inverse_z)


def complex_apply(data, cosine, sine, spec, sign):
    half = data.shape[-1] // 2
    real_part = data[..., :half]
    imag_part = data[..., half:]
    out_real = jnp.einsum(spec, real_part, cosine, precision=HIGH) - sign * jnp.einsum(
        spec, imag_part, sine, precision=HIGH
    )
    out_imag = jnp.einsum(spec, imag_part, cosine, precision=HIGH) + sign * jnp.einsum(
        spec, real_part, sine, precision=HIGH
    )
    return jnp.concatenate([out_real, out_imag], axis=-1)


def owner_step(grad_modes, input_modes, mode_weights):
    half = grad_modes.shape[-1] // 2
    g_real, g_imag = (grad_modes[..., :half], grad_modes[..., half:])
    x_real, x_imag = (input_modes[..., :half], input_modes[..., half:])
    w_real, w_imag = (mode_weights[..., :half], mode_weights[..., half:])
    f32 = jnp.float32
    spec_w = "bixyk,boxyk->ioxyk"
    dw_real = jnp.einsum(spec_w, x_real, g_real, preferred_element_type=f32) + jnp.einsum(
        spec_w, x_imag, g_imag, preferred_element_type=f32
    )
    dw_imag = jnp.einsum(spec_w, x_real, g_imag, preferred_element_type=f32) - jnp.einsum(
        spec_w, x_imag, g_real, preferred_element_type=f32
    )
    weight_grad = jnp.concatenate([dw_real, dw_imag], axis=-1).astype(jnp.bfloat16)
    spec_d = "ioxyk,boxyk->bixyk"
    dm_real = jnp.einsum(spec_d, w_real, g_real, preferred_element_type=f32) + jnp.einsum(
        spec_d, w_imag, g_imag, preferred_element_type=f32
    )
    dm_imag = jnp.einsum(spec_d, w_real, g_imag, preferred_element_type=f32) - jnp.einsum(
        spec_d, w_imag, g_real, preferred_element_type=f32
    )
    mode_grad = jnp.concatenate([dm_real, dm_imag], axis=-1).astype(jnp.bfloat16)
    return (weight_grad, mode_grad)


def body(out_grad, input_modes, mode_weights):
    grid_x = out_grad.shape[2] * lax.axis_size("px")
    grid_y = out_grad.shape[3] * lax.axis_size("py")
    grid_z = out_grad.shape[4]
    forward_z, inverse_z = z_tables(KZM, grid_z)
    cos_x, sin_x = twiddle_tables(kept_wavenumbers(KXM, grid_x), grid_x)
    cos_y, sin_y = twiddle_tables(kept_wavenumbers(KYM, grid_y), grid_y)
    grad_z = jnp.einsum("bcxyz,zk->bcxyk", out_grad, forward_z, precision=HIGH)
    lines_y = lax.all_to_all(grad_z, "py", split_axis=1, concat_axis=3, tiled=True)
    grad_y = complex_apply(lines_y, cos_y, sin_y, "bcxyk,qy->bcxqk", -1.0)
    lines_x = lax.all_to_all(grad_y, "px", split_axis=3, concat_axis=2, tiled=True)
    grad_modes = complex_apply(lines_x, cos_x, sin_x, "bcxqk,px->bcpqk", -1.0).astype(jnp.bfloat16)
    owned = lax.all_to_all(
        lax.all_to_all(grad_modes, "px", split_axis=2, concat_axis=3, tiled=True),
        "py",
        split_axis=3,
        concat_axis=1,
        tiled=True,
    )
    weight_grad, mode_grad = owner_step(owned, input_modes, mode_weights)
    returned = lax.all_to_all(
        lax.all_to_all(mode_grad, "py", split_axis=1, concat_axis=3, tiled=True),
        "px",
        split_axis=3,
        concat_axis=2,
        tiled=True,
    )
    back_x = complex_apply(returned.astype(jnp.float32), cos_x, sin_x, "bcpqk,px->bcxqk", 1.0)
    spread_x = lax.all_to_all(back_x, "px", split_axis=2, concat_axis=3, tiled=True)
    back_y = complex_apply(spread_x, cos_y, sin_y, "bcxqk,qy->bcxyk", 1.0)
    blocks = lax.all_to_all(back_y, "py", split_axis=3, concat_axis=1, tiled=True)
    input_grad = jnp.einsum("bcxyk,kz->bcxyz", blocks, inverse_z, precision=HIGH).astype(
        jnp.bfloat16
    )
    return (weight_grad, input_grad)


def solution(mesh):
    return jax.shard_map(
        body,
        mesh=mesh,
        in_specs=(
            P(None, None, "px", "py", None),
            P(None, None, "px", "py", None),
            P(None, None, "px", "py", None),
        ),
        out_specs=(P(None, None, "px", "py", None), P(None, None, "px", "py", None)),
        check_vma=False,
    )
```

profile of v0, /device:TPU:22, one launch (start us, length us, event | category | flops | bytes accessed | tf_op | source)
XLA Modules:
  0.0 695.2 jit_solution(7549930124198172443)
XLA Ops:
  0.7 13.7 %fusion.20 = f32[4,32,16,8,66]{4,1,3,2,0:T(8,128)S(1)} fusion(f32[4,32,16,8,128]{4,3,2,1,0:T(8,128)} %param.3, f32[128,33]{0,1:T(8,128)S(1)} %get-tuple-element.20, f32[128,33]{0,1:T(8,128)S(1)} %get-tuple-element.21), kind=kOutput, calls=%fused_computation.27 | convolution fusion | flops 1660952832 | bytes 12747776 | tf_op jit(solution)/shard_map/bcxyz,zk->bcxyk/dot_general | solution.py:82
  14.4 8.3 %copy.90 = f32[4,32,16,8,66]{4,3,2,0,1:T(8,128)} copy(f32[4,32,16,8,66]{4,1,3,2,0:T(8,128)S(1)} %fusion.20) | data formatting | bytes 8650752 | tf_op jit(solution)/shard_map/bcxyz,zk->bcxyk/dot_general | solution.py:82
  22.7 6.7 all-to-all-start
  29.3 94.9 %all-to-all-done = f32[4,32,16,8,66]{4,3,2,0,1:T(8,128)} async-done(((f32[4,32,16,8,66]{4,3,2,0,1:T(8,128)}), f32[4,32,16,8,66]{4,3,2,0,1:T(8,128)}, u32[]{:S(2)}, u32[]{:S(2)}) %all-to-all-start) | async-done | bytes 4325408 | tf_op jit(solution)/shard_map/all_to_all | solution.py:83
  124.2 4.5 copy.162
  128.7 15.5 %fusion.6 = f32[64,4,2,16,33]{0,4,3,2,1:T(8,128)S(1)} fusion(f32[4,2,16,128,66]{4,3,2,1,0:T(8,128)S(1)} %bitcast.137, s32[64]{0:T(128)S(1)} %compare_select_fusion), kind=kOutput, calls=%fused_computation.10 | convolution fusion | flops 415358976 | bytes 5406976 | tf_op jit(solution)/shard_map/bcxyk,qy->bcxqk/dot_general | solution.py:44
  144.3 15.6 %fusion.4 = f32[64,4,2,16,33]{0,4,3,2,1:T(8,128)S(1)} fusion(f32[4,2,16,128,66]{4,3,2,1,0:T(8,128)S(1)} %bitcast.138, s32[64]{0:T(128)S(1)} %compare_select_fusion), kind=kOutput, calls=%fused_computation.8 | convolution fusion | flops 415358976 | bytes 5406976 | tf_op jit(solution)/shard_map/bcxyk,qy->bcxqk/dot_general | solution.py:41
  159.8 13.8 %add_bitcast_fusion.1 = f32[4,2,16,64,33]{3,4,2,1,0:T(8,128)S(1)} fusion(f32[64,4,2,16,33]{0,4,3,2,1:T(8,128)S(1)} %fusion.6, f32[4,2,16,128,66]{4,3,2,1,0:T(8,128)S(1)} %bitcast.139, s32[64]{0:T(128)S(1)} %compare_select_fusion), kind=kOutput, calls=%fused_computation.31 | convolution fusion | flops 415899648 | bytes 6488320 | tf_op jit(solution)/shard_map/bcxyk,qy->bcxqk/dot_general | solution.py:44
  173.6 13.4 %subtract_bitcast_fusion.1 = f32[4,2,16,64,33]{3,4,2,1,0:T(8,128)S(1)} fusion(f32[64,4,2,16,33]{0,4,3,2,1:T(8,128)S(1)} %fusion.4, f32[4,2,16,128,66]{4,3,2,1,0:T(8,128)S(1)} %bitcast.140, s32[64]{0:T(128)S(1)} %compare_select_fusion), kind=kOutput, calls=%fused_computation.32 | convolution fusion | flops 415899648 | bytes 6488320 | tf_op jit(solution)/shard_map/bcxyk,qy->bcxqk/dot_general | solution.py:41
  187.1 2.8 pad_maximum_fusion.1
  189.8 6.5 copy.94
  196.3 53.7 %all_to_all.144 = f32[4,2,16,64,66]{4,2,1,0,3:T(8,128)S(1)} all-to-all(f32[4,2,16,64,66]{4,2,1,0,3:T(8,128)} %copy.94), channel_id=1, replica_groups=mesh['px'=8,'py'=16] {'px'}, dimensions={3} | all-to-all | bytes 4325376 | tf_op jit(solution)/shard_map/all_to_all | solution.py:85
  250.0 2.4 copy.96
  252.4 4.7 fusion.167
  257.2 2.9 copy.144
  260.1 2.4 fusion.62
  262.5 2.9 copy.143
  270.0 1.9 copy.99
  271.9 19.0 %all_to_all.145 = bf16[4,2,64,8,66]{4,3,1,0,2:T(8,128)(2,1)S(1)} all-to-all(bf16[4,2,64,8,66]{4,3,1,0,2:T(8,128)(2,1)S(1)} %copy.99), channel_id=1, replica_groups=mesh['px'=8,'py'=16] {'px'}, dimensions={2} | all-to-all | bytes 1081344 | tf_op jit(solution)/shard_map/all_to_all | solution.py:88
  291.2 1.7 copy.102
  292.8 3.8 all-to-all-start.3
  296.6 17.1 %fusion.166 = (bf16[32,32,8,4,33]{4,3,2,1,0:T(4,128)(2,1)}, bf16[32,32,8,4,33]{4,3,2,1,0:T(4,128)(2,1)}) fusion(bf16[32,32,8,4,66]{4,3,2,1,0:T(4,128)(2,1)} %param.5), kind=kLoop, calls=%fused_computation.198 | loop fusion | bytes 8650752 | tf_op jit(solution)/shard_map/slice | solution.py:54
  313.7 23.9 %copy.149 = bf16[32,32,8,4,33]{1,0,4,3,2:T(8,128)(2,1)} copy(bf16[32,32,8,4,33]{4,3,2,1,0:T(4,128)(2,1)} %get-tuple-element.11) | data formatting | bytes 4325376
  337.6 23.9 %copy.150 = bf16[32,32,8,4,33]{1,0,4,3,2:T(8,128)(2,1)} copy(bf16[32,32,8,4,33]{4,3,2,1,0:T(4,128)(2,1)} %get-tuple-element.10) | data formatting | bytes 4325376
  362.2 1.5 copy.147
  363.7 1.5 copy.145
  365.3 9.5 %fusion.174 = f32[8,4,33,4,32]{4,3,2,1,0:T(4,128)} fusion(bf16[4,32,8,4,33]{1,0,4,3,2:T(4,128)(2,1)S(1)} %copy.147, bf16[32,32,8,4,33]{1,0,4,3,2:T(8,128)(2,1)} %copy.149), kind=kOutput, calls=%fused_computation.206 | convolution fusion | flops 8650752 | bytes 2973696 | tf_op jit(solution)/shard_map/ioxyk,boxyk->bixyk/dot_general | solution.py:68
  374.8 8.0 %fusion.173 = f32[8,4,33,4,32]{4,3,2,1,0:T(4,128)S(1)} fusion(bf16[4,32,8,4,33]{1,0,4,3,2:T(4,128)(2,1)S(1)} %copy.145, bf16[32,32,8,4,33]{1,0,4,3,2:T(8,128)(2,1)} %copy.149), kind=kOutput, calls=%fused_computation.205 | convolution fusion | flops 8650752 | bytes 2973696 | tf_op jit(solution)/shard_map/ioxyk,boxyk->bixyk/dot_general | solution.py:65
  382.9 6.0 fusion.36
  388.9 4.8 fusion.35
  393.6 3.0 pad_maximum_fusion.4
  396.6 4.0 copy.113
  400.7 22.0 %all_to_all.146 = bf16[4,32,8,4,66]{4,2,3,0,1:T(8,128)(2,1)S(1)} all-to-all(bf16[4,32,8,4,66]{4,2,3,0,1:T(8,128)(2,1)S(1)} %copy.113), channel_id=1, replica_groups=mesh['px'=8,'py'=16] {'py'}, dimensions={1} | all-to-all | bytes 1081344 | tf_op jit(solution)/shard_map/all_to_all | solution.py:96
  423.1 19.2 %all_to_all.147 = bf16[4,2,8,64,66]{4,2,1,0,3:T(8,128)(2,1)S(1)} all-to-all(bf16[4,2,8,64,66]{4,2,1,0,3:T(8,128)(2,1)S(1)} %copy.116), channel_id=1, replica_groups=mesh['px'=8,'py'=16] {'px'}, dimensions={3} | all-to-all | bytes 1081344 | tf_op jit(solution)/shard_map/all_to_all | solution.py:95
  443.5 1.7 fusion.168
  445.2 1.9 copy.152
  447.2 1.9 fusion.58
  449.1 1.9 copy.151
  454.1 1.6 pad_maximum_fusion.3
  455.7 5.0 copy.121
  460.7 8.8 %all-to-all-start.6 = ((f32[4,2,128,8,66]{4,3,1,0,2:T(8,128)}), f32[4,2,128,8,66]{4,3,1,0,2:T(8,128)}, u32[]{:S(2)}, u32[]{:S(2)}) async-start(f32[4,2,128,8,66]{4,3,1,0,2:T(8,128)} %copy.121), calls=%async_computation.6 | async-start | bytes 8388608 | tf_op jit(solution)/shard_map/all_to_all | solution.py:103
  469.5 2.3 fusion.169
  471.8 3.0 copy.146
  474.8 4.3 copy.148
  479.1 46.1 %all-to-all-done.6 = f32[4,2,128,8,66]{4,3,1,0,2:T(8,128)} async-done(((f32[4,2,128,8,66]{4,3,1,0,2:T(8,128)}), f32[4,2,128,8,66]{4,3,1,0,2:T(8,128)}, u32[]{:S(2)}, u32[]{:S(2)}) %all-to-all-start.6) | async-done | bytes 2162720 | tf_op jit(solution)/shard_map/all_to_all | solution.py:103
  525.2 2.8 copy.163
  527.9 7.8 %fusion.14 = f32[128,4,2,16,33]{0,4,3,2,1:T(8,128)S(1)} fusion(f32[4,2,16,64,66]{4,3,2,1,0:T(8,128)S(1)} %bitcast.141, s32[64]{0:T(128)S(1)} %compare_select_fusion), kind=kOutput, calls=%fused_computation.21 | convolution fusion | flops 415358976 | bytes 4325632 | tf_op jit(solution)/shard_map/bcxqk,qy->bcxyk/dot_general | solution.py:44
  535.7 8.4 %fusion.12 = f32[128,4,2,16,33]{0,4,3,2,1:T(8,128)S(1)} fusion(f32[4,2,16,64,66]{4,3,2,1,0:T(8,128)S(1)} %bitcast.142, s32[64]{0:T(128)S(1)} %compare_select_fusion), kind=kOutput, calls=%fused_computation.19 | convolution fusion | flops 415358976 | bytes 4325632 | tf_op jit(solution)/shard_map/bcxqk,qy->bcxyk/dot_general | solution.py:41
  544.2 6.8 add_bitcast_fusion
  551.0 7.0 %subtract_bitcast_fusion = f32[4,2,16,128,33]{3,4,2,1,0:T(8,128)S(1)} fusion(f32[128,4,2,16,33]{0,4,3,2,1:T(8,128)S(1)} %fusion.12, f32[4,2,16,64,66]{4,3,2,1,0:T(8,128)S(1)} %bitcast.144, s32[64]{0:T(128)S(1)} %compare_select_fusion), kind=kOutput, calls=%fused_computation.30 | convolution fusion | flops 415899648 | bytes 6488320 | tf_op jit(solution)/shard_map/bcxqk,qy->bcxyk/dot_general | solution.py:41
  558.0 2.6 pad_maximum_fusion.2
  560.6 9.1 %copy.126 = f32[4,2,16,128,66]{4,2,1,0,3:T(8,128)} copy(f32[4,2,16,128,66]{3,4,2,1,0:T(8,128)} %pad_maximum_fusion.2) | data formatting | bytes 8650752 | tf_op jit(solution)/shard_map/concatenate | solution.py:47
  569.7 9.9 %all-to-all-start.7 = ((f32[4,2,16,128,66]{4,2,1,0,3:T(8,128)}), f32[4,2,16,128,66]{4,2,1,0,3:T(8,128)}, u32[]{:S(2)}, u32[]{:S(2)}) async-start(f32[4,2,16,128,66]{4,2,1,0,3:T(8,128)} %copy.126), calls=%async_computation.7 | async-start | bytes 16777216 | tf_op jit(solution)/shard_map/all_to_all | solution.py:105
  579.8 7.0 %fusion.172 = f32[8,4,33,32,32]{4,3,2,1,0:T(8,128)} fusion(bf16[4,32,8,4,33]{1,0,4,3,2:T(4,128)(2,1)S(1)} %copy.147, bf16[4,32,8,4,33]{1,0,4,3,2:T(4,128)(2,1)S(1)} %copy.146), kind=kOutput, calls=%fused_computation.204 | convolution fusion | flops 8650752 | bytes 4866048 | tf_op jit(solution)/shard_map/bixyk,boxyk->ioxyk/dot_general | solution.py:60
  586.8 11.4 %fusion.1 = bf16[32,32,8,4,33]{0,1,4,3,2:T(8,128)(2,1)} fusion(f32[8,4,33,32,32]{4,3,2,1,0:T(8,128)} %fusion.172, bf16[4,32,8,4,33]{1,0,4,3,2:T(4,128)(2,1)S(1)} %copy.145, bf16[4,32,8,4,33]{1,0,4,3,2:T(4,128)(2,1)S(1)} %copy-done), kind=kOutput, calls=%fused_computation.3 | convolution fusion | flops 10813440 | bytes 7028736 | tf_op jit(solution)/shard_map/bixyk,boxyk->ioxyk/dot_general | solution.py:60
  598.2 20.4 %copy.110 = bf16[32,32,8,4,33]{4,2,3,1,0:T(8,128)(2,1)} copy(bf16[32,32,8,4,33]{0,1,4,3,2:T(8,128)(2,1)} %fusion.1) | data formatting | bytes 4325376 | tf_op jit(solution)/shard_map/sub | solution.py:60
  618.6 7.0 %fusion.171 = f32[8,4,33,32,32]{4,3,2,1,0:T(8,128)} fusion(bf16[4,32,8,4,33]{1,0,4,3,2:T(4,128)(2,1)S(1)} %copy.145, bf16[4,32,8,4,33]{1,0,4,3,2:T(4,128)(2,1)S(1)} %copy.146), kind=kOutput, calls=%fused_computation.203 | convolution fusion | flops 8650752 | bytes 4866048 | tf_op jit(solution)/shard_map/bixyk,boxyk->ioxyk/dot_general | solution.py:57
  625.6 11.4 %fusion = bf16[32,32,8,4,33]{0,1,4,3,2:T(8,128)(2,1)} fusion(f32[8,4,33,32,32]{4,3,2,1,0:T(8,128)} %fusion.171, bf16[4,32,8,4,33]{1,0,4,3,2:T(4,128)(2,1)S(1)} %copy.147, bf16[4,32,8,4,33]{1,0,4,3,2:T(4,128)(2,1)S(1)} %copy-done.1), kind=kOutput, calls=%fused_computation.2 | convolution fusion | flops 10813440 | bytes 7028736 | tf_op jit(solution)/shard_map/bixyk,boxyk->ioxyk/dot_general | solution.py:57
  637.0 20.5 %copy.109 = bf16[32,32,8,4,33]{4,2,3,1,0:T(8,128)(2,1)} copy(bf16[32,32,8,4,33]{0,1,4,3,2:T(8,128)(2,1)} %fusion) | data formatting | bytes 4325376 | tf_op jit(solution)/shard_map/add | solution.py:57
  657.5 8.2 %pad_maximum_fusion = bf16[32,32,8,4,66]{4,2,3,1,0:T(8,128)(2,1)S(1)} fusion(bf16[32,32,8,4,33]{4,2,3,1,0:T(8,128)(2,1)} %copy.110, bf16[32,32,8,4,33]{4,2,3,1,0:T(8,128)(2,1)} %copy.109), kind=kLoop, calls=%fused_computation.4 | loop fusion | flops 8650752 | bytes 8650752 | tf_op jit(solution)/shard_map/concatenate | solution.py:63
  665.7 6.1 copy.129
  671.8 3.2 all-to-all-done.7
  675.0 11.5 %copy.128 = f32[4,16,2,16,8,66]{5,4,3,2,1,0:T(8,128)S(1)} copy(f32[4,16,2,16,8,66]{5,3,2,0,4,1:T(8,128)} %bitcast.51) | data formatting | bytes 8650752 | tf_op jit(solution)/shard_map/all_to_all | solution.py:105
  686.5 8.4 %convolution_convert_fusion = bf16[4,32,16,8,128]{4,3,2,1,0:T(8,128)(2,1)} fusion(f32[4,32,16,8,66]{4,3,2,1,0:T(8,128)S(1)} %bitcast.148, f32[33,128]{1,0:T(8,128)S(1)} %get-tuple-element.22, f32[33,128]{1,0:T(8,128)S(1)} %get-tuple-element.23), kind=kOutput, calls=%fused_computation.28 | convolution fusion | flops 1663049984 | bytes 8553472 | tf_op jit(solution)/shard_map/bcxyk,kz->bcxyz/dot_general | solution.py:106
  (36 shorter events, 10.4 us)
Async XLA Ops:
  22.7 101.5 %all-to-all-start = ((f32[4,32,16,8,66]{4,3,2,0,1:T(8,128)}), f32[4,32,16,8,66]{4,3,2,0,1:T(8,128)}, u32[]{:S(2)}, u32[]{:S(2)}) async-start(f32[4,32,16,8,66]{4,3,2,0,1:T(8,128)} %copy.90), calls=%async_computation | async-start | bytes 16777216 | tf_op jit(solution)/shard_map/all_to_all | solution.py:83
  265.4 1.4 copy-start.2
  292.8 68.7 %all-to-all-start.3 = ((bf16[4,2,8,64,66]{4,2,1,0,3:T(8,128)(2,1)}), bf16[4,2,8,64,66]{4,2,1,0,3:T(8,128)(2,1)S(1)}, u32[]{:S(2)}, u32[]{:S(2)}) async-start(bf16[4,2,8,64,66]{4,2,1,0,3:T(8,128)(2,1)} %copy.102), calls=%async_computation.3 | async-start | bytes 2097152 | tf_op jit(solution)/shard_map/all_to_all | solution.py:87
  365.3 17.6 %slice-start = ((s8[8650752]{0:T(1024)(128)(4,1)}), s8[4194304]{0:T(1024)(128)(4,1)S(1)}, s32[]{:S(2)}) async-start(s8[8650752]{0:T(1024)(128)(4,1)} %bitcast.145), calls=%async_computation.8 | async-start | bytes 8388608
  365.3 17.6 %slice-start.1 = ((s8[8650752]{0:T(1024)(128)(4,1)}), s8[4194304]{0:T(1024)(128)(4,1)S(1)}, s32[]{:S(2)}) async-start(s8[8650752]{0:T(1024)(128)(4,1)} %bitcast.145), calls=%async_computation.9 | async-start | bytes 8388608
  374.8 8.1 %slice-start.2 = ((s8[8650752]{0:T(1024)(128)(4,1)}), s8[262144]{0:T(1024)(128)(4,1)S(1)}, s32[]{:S(2)}) async-start(s8[8650752]{0:T(1024)(128)(4,1)} %bitcast.145), calls=%async_computation.10 | async-start | bytes 524288
  451.0 1.3 copy-start.3
  460.7 8.8 %copy-start.4 = (bf16[4,32,8,4,66]{4,3,2,1,0:T(4,128)(2,1)S(1)}, bf16[4,32,8,4,66]{4,3,2,1,0:T(4,128)(2,1)}, u32[]{:S(2)}) copy-start(bf16[4,32,8,4,66]{4,3,2,1,0:T(4,128)(2,1)} %param.4) | copy-start | bytes 1622020
  460.7 64.5 %all-to-all-start.6 = ((f32[4,2,128,8,66]{4,3,1,0,2:T(8,128)}), f32[4,2,128,8,66]{4,3,1,0,2:T(8,128)}, u32[]{:S(2)}, u32[]{:S(2)}) async-start(f32[4,2,128,8,66]{4,3,1,0,2:T(8,128)} %copy.121), calls=%async_computation.6 | async-start | bytes 8388608 | tf_op jit(solution)/shard_map/all_to_all | solution.py:103
  569.7 105.3 %all-to-all-start.7 = ((f32[4,2,16,128,66]{4,2,1,0,3:T(8,128)}), f32[4,2,16,128,66]{4,2,1,0,3:T(8,128)}, u32[]{:S(2)}, u32[]{:S(2)}) async-start(f32[4,2,16,128,66]{4,2,1,0,3:T(8,128)} %copy.126), calls=%async_computation.7 | async-start | bytes 16777216 | tf_op jit(solution)/shard_map/all_to_all | solution.py:105
  579.8 7.0 %copy-start = (bf16[4,32,8,4,33]{1,0,4,3,2:T(4,128)(2,1)S(1)}, bf16[4,32,8,4,33]{1,0,4,3,2:T(4,128)(2,1)}, u32[]{:S(2)}) copy-start(bf16[4,32,8,4,33]{1,0,4,3,2:T(4,128)(2,1)} %copy.148) | copy-start | bytes 811012
  618.6 7.0 %copy-start.1 = (bf16[4,32,8,4,33]{1,0,4,3,2:T(4,128)(2,1)S(1)}, bf16[4,32,8,4,33]{1,0,4,3,2:T(4,128)(2,1)}, u32[]{:S(2)}) copy-start(bf16[4,32,8,4,33]{1,0,4,3,2:T(4,128)(2,1)} %copy.148) | copy-start | bytes 811012
where the time goes:
time: 705 us; the launch traced here: 695 us
  local copies, waits for them, and re-layouts  201 us (29%)
  matrix products  187 us (27%)
  waiting for transfers between devices  144 us (20%)
  blocking collectives  114 us (16%)
  starting transfers between devices  29.2 us (4%)
  other arithmetic  18.9 us (3%)
    all_to_all x1, waiting for transfers between devices, body(): lax.all_to_all(grad_z, 'py', split_axis=1, concat_axis=3, tiled=True)  94.9 us
    unnamed x27, local copies, waits for them, and re-layouts  74.4 us
    all_to_all x1, blocking collectives, body(): lax.all_to_all(grad_y, 'px', split_axis=3, concat_axis=2, tiled=True)  53.7 us
    all_to_all x1, waiting for transfers between devices, body(): lax.all_to_all(back_x, 'px', split_axis=2, concat_axis=3, tiled=True)  46.1 us
    dot_general x4, matrix products, complex_apply(): jnp.einsum(spec, imag_part, cosine, precision=HIGH)  27.7 us
    dot_general x4, matrix products, complex_apply(): jnp.einsum(spec, imag_part, sine, precision=HIGH)  26.2 us
    dot_general x4, matrix products, complex_apply(): jnp.einsum(spec, real_part, sine, precision=HIGH)  22.9 us
    dot_general x4, matrix products, complex_apply(): jnp.einsum(spec, real_part, cosine, precision=HIGH)  22.6 us
  transfers between devices with their start and end apart: 4, of which 3 were waited for; matrix products, arithmetic and copies ran while one was open for 24% of the time, Pallas kernels for 0%

commit v1 on v0

v1 whole, which is shorter than its diff:
```python
import math

import jax
import jax.numpy as jnp
import ml_dtypes
import numpy as np
from jax import lax
from jax.experimental import pallas as pl
from jax.experimental.pallas import tpu as pltpu
from jax.sharding import PartitionSpec as P

BF = jnp.bfloat16
F32 = jnp.float32
MESH = pl.DeviceIdType.MESH
N = 128
KEPT = 64
KZ = 33
PX = 8
PY = 16
MR = 144
CR = 272
T1, T2, G, GS = 0, 16, 32, 48


def split(table):
    high = table.astype(ml_dtypes.bfloat16)
    low = (table - high.astype(np.float64)).astype(ml_dtypes.bfloat16)
    return high, low


def tables():
    bf = ml_dtypes.bfloat16
    grid = np.arange(N)
    angle_z = 2 * math.pi * (np.outer(np.arange(KZ), grid) % N) / N
    norm = 1.0 / math.sqrt(N)
    cz, sz = np.cos(angle_z) * norm, np.sin(angle_z) * norm
    kept = np.concatenate([np.arange(KEPT // 2), np.arange(N - KEPT // 2, N)])
    angle = 2 * math.pi * (np.outer(kept, grid) % N) / N
    cos, sin = np.cos(angle) * norm, np.sin(angle) * norm

    fz = np.stack([cz, -sz], axis=1).reshape(2 * KZ, N)
    hi, lo = split(fz)
    zf = np.zeros((144, 256), bf)
    zf[:66, :128] = hi
    zf[:66, 128:] = hi
    zf[72:138, :128] = lo
    weight = np.where(np.arange(KZ) == 0, 1.0, 2.0)[:, None]
    iz = np.stack([weight * cz, -weight * sz], axis=1).reshape(2 * KZ, N)
    hi, lo = split(iz)
    zi = np.zeros((2, 72, N), bf)
    zi[0, :66] = hi
    zi[1, :66] = lo

    full = np.zeros((2, KEPT, 2, N))
    full[0, :, 0] = cos
    full[0, :, 1] = sin
    full[1, :, 0] = -sin
    full[1, :, 1] = cos

    wy = full.reshape(2, PX, 8, 2, PY, 8).transpose(1, 0, 2, 4, 3, 5).reshape(128, 256)
    hi, lo = split(wy)
    yf = np.concatenate([hi, lo], axis=0)
    yi = np.concatenate([hi.T, lo.T], axis=1)

    wx = full.reshape(2, PX, 8, 2, PX, 16).transpose(3, 4, 5, 1, 0, 2)
    hi, lo = split(wx)
    xf = np.zeros((2, 2, PX, 8, 16, PX, 2, 8, 8), bf)
    for bc in range(8):
        xf[0, :, :, bc, :, :, :, bc, :] = hi
        xf[1, :, :, bc, :, :, :, bc, :] = lo
    xf = xf.reshape(2, 2048, 1024)

    perm = np.zeros((2, MR, CR), bf)
    for h in range(2):
        for k in range(KZ):
            for r in range(4):
                perm[h, 4 * k + r, 8 * k + 4 * h + r] = 1
    perm = perm.reshape(2 * MR, CR)
    permt = np.ascontiguousarray(perm.T)

    place = np.zeros((2, MR, 4, 2, 128), bf)
    back = np.zeros((MR, 4, 128), bf)
    for k in range(KZ):
        for r in range(4):
            place[0, 4 * k + r, r, 0, k] = 1
            place[1, 4 * k + r, r, 0, KZ + k] = 1
            place[1, 4 * k + r, r, 1, k] = 1
            place[0, 4 * k + r, r, 1, KZ + k] = -1
            back[4 * k + r, r, k] = 1
    place = place.reshape(2, MR, 1024)
    back = back.reshape(MR, 512)

    dup = np.zeros((2 * KZ, 2, 128), bf)
    for k in range(KZ):
        for part in range(2):
            dup[part * KZ + k, part, k] = 1
            dup[part * KZ + k, part, KZ + k] = 1
    dup = dup.reshape(2 * KZ, 256)
    return zf, zi, yf, yi, xf, perm, permt, place, back, dup


def dot(a, b):
    return jnp.dot(a, b, preferred_element_type=F32)


def dot_nt(a, b):
    return lax.dot_general(a, b, (((1,), (1,)), ((), ())), preferred_element_type=F32)


def kernel(
    og, xm, w_hbm, xf_hbm, zf, zi, yf, yi, perm, permt, place, back, dup,
    wg, ig,
    ogv, wv, xfv, send_a, recv_a, send_b, recv_b, send_m, recv_m, send_n, recv_n,
    lines, dm, xr, xi, blk, turn, outv,
    og_sem, w_sem, xf_sem, wg_sem, ig_sem, self_sem,
    sa_sem, ra_sem, sb_sem, rb_sem, sm_sem, rm_sem,
    sn_sem, rn_sem, sc_sem, rc_sem, sd_sem, rd_sem,
):
    px = lax.axis_index("px")
    py = lax.axis_index("py")
    owner_px = py // 2

    for k in range(PY):
        chunk = lax.rem(py + 1 + k, PY)
        pltpu.make_async_copy(og.at[:, chunk], ogv.at[pl.ds(chunk * 4, 4)], og_sem.at[chunk]).start()
    pltpu.make_async_copy(xf_hbm, xfv, xf_sem).start()
    pltpu.make_async_copy(w_hbm, wv, w_sem).start()

    barrier = pltpu.get_barrier_semaphore()
    mine = jnp.where(owner_px == px, 1, 0)

    def greet_py(s, c):
        pl.semaphore_signal(barrier, inc=1, device_id=(px, lax.rem(py + s, PY)), device_id_type=MESH)
        return c

    def greet_px(s, c):
        pl.semaphore_signal(barrier, inc=1, device_id=(lax.rem(px + s, PX), py), device_id_type=MESH)
        return c

    def greet_m(t, c):
        to_x, to_y = t // 2, 2 * px + lax.rem(t, 2)

        @pl.when(jnp.logical_not(jnp.logical_and(to_x == px, to_y == py)))
        def _():
            pl.semaphore_signal(barrier, inc=1, device_id=(to_x, to_y), device_id_type=MESH)

        @pl.when(jnp.logical_not(jnp.logical_and(owner_px == px, t == py)))
        def _():
            pl.semaphore_signal(barrier, inc=1, device_id=(owner_px, t), device_id_type=MESH)

        return c

    lax.fori_loop(1, PY, greet_py, 0)
    lax.fori_loop(1, PX, greet_px, 0)
    lax.fori_loop(0, PY, greet_m, 0)

    def copy_a(s):
        to = lax.rem(py + s, PY)
        return pltpu.make_async_remote_copy(
            src_ref=send_a.at[to], dst_ref=recv_a.at[py], send_sem=sa_sem.at[to], recv_sem=ra_sem.at[py],
            device_id=(px, to), device_id_type=MESH)

    def arrive_a(src):
        return pltpu.make_async_remote_copy(
            src_ref=send_a.at[src], dst_ref=recv_a.at[src], send_sem=sa_sem.at[src], recv_sem=ra_sem.at[src],
            device_id=(px, src), device_id_type=MESH)

    def copy_b(s):
        to = lax.rem(px + s, PX)
        return pltpu.make_async_remote_copy(
            src_ref=send_b.at[to], dst_ref=recv_b.at[px], send_sem=sb_sem.at[to], recv_sem=rb_sem.at[px],
            device_id=(to, py), device_id_type=MESH)

    def arrive_b(src):
        return pltpu.make_async_remote_copy(
            src_ref=send_b.at[src], dst_ref=recv_b.at[src], send_sem=sb_sem.at[src], recv_sem=rb_sem.at[src],
            device_id=(src, py), device_id_type=MESH)

    def copy_m(to_x, h):
        return pltpu.make_async_remote_copy(
            src_ref=send_m.at[to_x, h], dst_ref=recv_m.at[py], send_sem=sm_sem.at[to_x, h], recv_sem=rm_sem.at[py],
            device_id=(to_x, 2 * px + h), device_id_type=MESH)

    def copy_n(to_y):
        h = lax.rem(py, 2)
        return pltpu.make_async_remote_copy(
            src_ref=send_n.at[to_y], dst_ref=recv_n.at[px, h], send_sem=sn_sem.at[to_y], recv_sem=rn_sem.at[px, h],
            device_id=(owner_px, to_y), device_id_type=MESH)

    def copy_c(s):
        to = lax.rem(px + s, PX)
        return pltpu.make_async_remote_copy(
            src_ref=send_b.at[PX + to], dst_ref=recv_b.at[PX + px], send_sem=sc_sem.at[to], recv_sem=rc_sem.at[px],
            device_id=(to, py), device_id_type=MESH)

    def arrive_c(src):
        return pltpu.make_async_remote_copy(
            src_ref=send_b.at[PX + src], dst_ref=recv_b.at[PX + src], send_sem=sc_sem.at[src], recv_sem=rc_sem.at[src],
            device_id=(src, py), device_id_type=MESH)

    def copy_d(s):
        to = lax.rem(py + s, PY)
        return pltpu.make_async_remote_copy(
            src_ref=send_a.at[PY + to], dst_ref=recv_a.at[PY + py], send_sem=sd_sem.at[to], recv_sem=rd_sem.at[py],
            device_id=(px, to), device_id_type=MESH)

    def arrive_d(src):
        return pltpu.make_async_remote_copy(
            src_ref=send_a.at[PY + src], dst_ref=recv_a.at[PY + src], send_sem=sd_sem.at[src], recv_sem=rd_sem.at[src],
            device_id=(px, src), device_id_type=MESH)

    def z_forward(chunk):
        pltpu.make_async_copy(og.at[:, chunk], ogv.at[pl.ds(chunk * 4, 4)], og_sem.at[chunk]).wait()
        for jj in range(4):
            parts = []
            for j in (2 * jj, 2 * jj + 1):
                for b in range(4):
                    parts.append(ogv[chunk * 4 + b, pl.ds(j, 32, stride=8), :])
            rows = jnp.concatenate(parts, axis=0)
            high = rows.astype(BF)
            low = (rows - high.astype(F32)).astype(BF)
            both = dot_nt(zf[...], jnp.concatenate([high, low], axis=1))
            res = both[0:72] + both[72:144]
            blk[pl.ds(2 * jj, 72, stride=8), :] = res[:, 0:128]
            blk[pl.ds(2 * jj + 1, 72, stride=8), :] = res[:, 128:256]

    def step_a(s, c):
        to = lax.rem(py + s, PY)
        z_forward(to)
        send_a[to] = blk[0:528, :].reshape(KZ, 16, 128).astype(BF)

        @pl.when(s == 1)
        def _():
            pl.semaphore_wait(barrier, 15 + 7 + 32 - 2 * mine)

        copy_a(s).start()
        return c

    lax.fori_loop(1, PY, step_a, 0)
    z_forward(py)
    recv_a[py] = blk[0:528, :].reshape(KZ, 16, 128).astype(BF)

    def widen(k, c):
        rows = pl.ds(pl.multiple_of(k * 256, 256), 256)
        both = dot(xm[rows, :], dup[...])
        xr[rows, :] = both[:, 0:128]
        xi[rows, :] = both[:, 128:256]
        ogv[T1 + k] = jnp.zeros((256, 128), F32)
        ogv[T2 + k] = jnp.zeros((256, 128), F32)
        return c

    lax.fori_loop(0, 16, widen, 0)

    def wait_a(s, c):
        arrive_a(lax.rem(py + PY - s, PY)).wait_recv()
        return c

    lax.fori_loop(1, PY, wait_a, 0)

    def step_b(k, c):
        data = recv_a[0:PY, k].reshape(256, 128)
        both = dot(yf[...], data)
        res = (both[0:128] + both[128:256]).astype(BF)
        send_b[0:PX, k] = res.reshape(PX, 16, 128)
        return c

    lax.fori_loop(0, KZ, step_b, 0, unroll=3)

    def start_b(s, c):
        copy_b(s).start()
        return c

    lax.fori_loop(1, PX, start_b, 0)
    pltpu.make_async_copy(xf_hbm, xfv, xf_sem).wait()

    def gather_b(src, data):
        data = data.astype(F32).reshape(KZ, 2, 8, 128)
        for ri in range(2):
            part = jnp.concatenate([data[:, ri].reshape(264, 128), jnp.zeros((8, 128), F32)], axis=0)
            lines[:, pl.ds(pl.multiple_of((ri * PX + src) * 128, 128), 128)] = part.astype(BF)

    def step_gather(s, c):
        src = lax.rem(px + PX - s, PX)
        arrive_b(src).wait_recv()
        gather_b(src, recv_b[src])
        return c

    gather_b(px, send_b[px])
    lax.fori_loop(1, PX, step_gather, 0)

    def step_c(k, c):
        cols = pl.ds(pl.multiple_of(k * 256, 256), 256)
        res = dot(lines[...], xfv[0, :, cols]) + dot(lines[...], xfv[1, :, cols])
        moved = dot(perm[...], res.astype(BF)).astype(BF)
        for e in range(2):
            send_m[2 * k + e] = moved[:, e * 128:(e + 1) * 128].reshape(2, MR, 128)
        for e in range(2):
            for h in range(2):
                own = jnp.logical_and(2 * k + e == px, 2 * px + h == py)

                @pl.when(jnp.logical_not(own))
                def _():
                    copy_m(2 * k + e, h).start()

                @pl.when(own)
                def _():
                    local = pltpu.make_async_copy(send_m.at[2 * k + e, h], recv_m.at[py], self_sem)
                    local.start()
                    local.wait()
        return c

    lax.fori_loop(0, 4, step_c, 0)

    def step_place(src, c):
        @pl.when(jnp.logical_not(jnp.logical_and(owner_px == px, src == py)))
        def _():
            pltpu.make_async_remote_copy(
                src_ref=send_m.at[0, 0], dst_ref=recv_m.at[src], send_sem=sm_sem.at[0, 0], recv_sem=rm_sem.at[src],
                device_id=(owner_px, src), device_id_type=MESH).wait_recv()

        turned = recv_m[src].astype(F32).T.astype(BF)
        res = dot(turned[0:64], place[0]) + dot(turned[64:128], place[1])
        for r in range(4):
            rows = pl.ds(r, 64, stride=4)
            ogv[G + src, rows, :] = res[:, r * 256:r * 256 + 128]
            ogv[GS + src, rows, :] = res[:, r * 256 + 128:r * 256 + 256]
        return c

    lax.fori_loop(0, PY, step_place, 0)
    pltpu.make_async_copy(w_hbm, wv, w_sem).wait()

    def step_modes(k, c):
        pair, half = k // 2, lax.rem(k, 2)
        off = pl.multiple_of(half * 16, 16)

        def add(op, acc):
            acc = list(acc)
            for oo in range(2):
                w = [wv[2 * pair + ii, 2 * op + oo, pl.ds(off, 16), :].astype(F32) for ii in range(2)]
                for b in range(4):
                    rows = pl.ds(pl.multiple_of((b * 2 + oo) * 32 + off, 16), 16)
                    gb = ogv[G + op, rows, 0:66]
                    sb = ogv[GS + op, rows, 0:66]
                    for ii in range(2):
                        n = (ii * 4 + b) * 2
                        acc[n] = acc[n] + w[ii] * gb
                        acc[n + 1] = acc[n + 1] + w[ii] * sb
            return tuple(acc)

        acc = lax.fori_loop(0, 16, add, tuple(jnp.zeros((16, 66), F32) for _ in range(16)))
        for ii in range(2):
            for b in range(4):
                rows = pl.ds(pl.multiple_of((b * 2 + ii) * 32 + off, 16), 16)
                ogv[T1 + pair, rows, 0:66] = acc[(ii * 4 + b) * 2]
                ogv[T2 + pair, rows, 0:66] = acc[(ii * 4 + b) * 2 + 1]
        return c

    def step_return(k, c):
        def rows_of(base, r):
            data = ogv[base + k, pl.ds(r, 64, stride=4), :]
            return data + pltpu.roll(data, 128 - KZ, 1)

        total = jnp.zeros((MR, 128), F32)
        for r in range(4):
            both = jnp.concatenate([rows_of(T1, r), rows_of(T2, r)], axis=0).astype(BF)
            total = total + dot_nt(back[:, r * 128:(r + 1) * 128], both)
        send_n[k] = total.astype(BF)
        own = jnp.logical_and(owner_px == px, k == py)

        @pl.when(jnp.logical_not(own))
        def _():
            copy_n(k).start()

        @pl.when(own)
        def _():
            local = pltpu.make_async_copy(send_n.at[k], recv_n.at[px, lax.rem(py, 2)], self_sem)
            local.start()
            local.wait()

        return c

    def step_pair(k, c):
        step_modes(2 * k, 0)
        step_modes(2 * k + 1, 0)
        return step_return(k, c)

    lax.fori_loop(0, 16, step_pair, 0)

    def step_weight(k, c):
        i, half = k // 2, lax.rem(k, 2)
        off = pl.multiple_of(half * 16, 16)
        xrb = [xr[pl.ds(pl.multiple_of((b * 32 + i) * 32 + off, 16), 16), 0:66] for b in range(4)]
        xib = [xi[pl.ds(pl.multiple_of((b * 32 + i) * 32 + off, 16), 16), 0:66] for b in range(4)]

        def one(op, c2):
            for oo in range(2):
                total = None
                for b in range(4):
                    rows = pl.ds(pl.multiple_of((b * 2 + oo) * 32 + off, 16), 16)
                    term = xrb[b] * ogv[G + op, rows, 0:66] + xib[b] * ogv[GS + op, rows, 0:66]
                    total = term if total is None else total + term
                wv[i, 2 * op + oo, pl.ds(off, 16), :] = total.astype(BF)
            return c2

        lax.fori_loop(0, 16, one, 0)

        @pl.when(half == 1)
        def _():
            pltpu.make_async_copy(wv.at[i], wg.at[i], wg_sem.at[i]).start()

        return c

    lax.fori_loop(0, 22, step_weight, 0)

    def step_unplace(k, c):
        for h in range(2):
            @pl.when(jnp.logical_not(jnp.logical_and(k == px, 2 * px + h == py)))
            def _():
                pltpu.make_async_remote_copy(
                    src_ref=send_n.at[0], dst_ref=recv_n.at[k, h], send_sem=sn_sem.at[0], recv_sem=rn_sem.at[k, h],
                    device_id=(k, 2 * px + h), device_id_type=MESH).wait_recv()

        moved = dot(permt[...], recv_n[k].reshape(2 * MR, 128))
        dm[:, pl.ds(pl.multiple_of(k * 128, 128), 128)] = moved.astype(BF)
        return c

    lax.fori_loop(0, PX, step_unplace, 0)

    def x_inverse(to):
        parts = []
        for ri in range(2):
            rows = pl.ds(pl.multiple_of((ri * PX + to) * 128, 128), 128)
            res = dot_nt(dm[...], xfv[0, rows, :]) + dot_nt(dm[...], xfv[1, rows, :])
            parts.append(res[0:264].reshape(KZ, 8, 128))
        return jnp.concatenate(parts, axis=1).astype(BF)

    def step_cb(s, c):
        to = lax.rem(px + s, PX)
        send_b[PX + to] = x_inverse(to)
        copy_c(s).start()
        return c

    lax.fori_loop(1, PX, step_cb, 0)
    recv_b[PX + px] = x_inverse(px)

    lax.fori_loop(22, 44, step_weight, 0)

    def wait_c(s, c):
        arrive_c(lax.rem(px + PX - s, PX)).wait_recv()
        return c

    lax.fori_loop(1, PX, wait_c, 0)

    def step_bb(k, c):
        data = recv_b[PX:2 * PX, k].reshape(128, 128)
        res = dot(yi[...], jnp.concatenate([data, data], axis=0)).astype(BF)
        send_a[PY:2 * PY, k] = res.reshape(PY, 16, 128)
        return c

    lax.fori_loop(0, KZ, step_bb, 0, unroll=3)

    def start_d(s, c):
        copy_d(s).start()
        return c

    lax.fori_loop(1, PY, start_d, 0)
    lax.fori_loop(44, 64, step_weight, 0)

    blk[528:576, :] = jnp.zeros((48, 128), F32)

    def z_inverse(src, data):
        blk[0:528, :] = data.astype(F32).reshape(528, 128)
        for j in range(8):
            turned = blk[pl.ds(j, 72, stride=8), :].T.astype(BF)
            res = dot(turned, zi[0]) + dot(turned, zi[1])
            turn[pl.ds(j, 128, stride=8), :] = res
        outv[src] = turn[...].reshape(4, 256, 128).astype(BF)
        pltpu.make_async_copy(outv.at[src], ig.at[:, src], ig_sem.at[src]).start()

    z_inverse(py, send_a[PY + py])

    def step_d(s, c):
        src = lax.rem(py + PY - s, PY)
        arrive_d(src).wait_recv()
        z_inverse(src, recv_a[PY + src])
        return c

    lax.fori_loop(1, PY, step_d, 0)

    def end_px(s, c):
        copy_b(s).wait_send()
        copy_c(s).wait_send()
        return c

    def end_py(s, c):
        copy_a(s).wait_send()
        copy_d(s).wait_send()
        return c

    def end_m(t, c):
        to_x, h = t // 2, lax.rem(t, 2)

        @pl.when(jnp.logical_not(jnp.logical_and(to_x == px, 2 * px + h == py)))
        def _():
            copy_m(to_x, h).wait_send()

        @pl.when(jnp.logical_not(jnp.logical_and(owner_px == px, t == py)))
        def _():
            copy_n(t).wait_send()

        pltpu.make_async_copy(outv.at[t], ig.at[:, t], ig_sem.at[t]).wait()
        return c

    def end_w(i, c):
        pltpu.make_async_copy(wv.at[i], wg.at[i], wg_sem.at[i]).wait()
        return c

    lax.fori_loop(1, PX, end_px, 0)
    lax.fori_loop(1, PY, end_py, 0)
    lax.fori_loop(0, PY, end_m, 0)
    lax.fori_loop(0, 32, end_w, 0)


def body(out_grad, input_modes, mode_weights):
    zf, zi, yf, yi, xf, perm, permt, place, back, dup = (jnp.asarray(t) for t in tables())
    og = out_grad.reshape(4, PY, 256, 128)
    xm = input_modes.reshape(4096, 66)
    w = mode_weights.reshape(32, 32, 32, 66)
    any_spec = pl.BlockSpec(memory_space=pl.ANY)
    vmem = pl.BlockSpec(memory_space=pltpu.VMEM)
    dma = pltpu.SemaphoreType.DMA
    wg, ig = pl.pallas_call(
        kernel,
        out_shape=(
            jax.ShapeDtypeStruct((32, 32, 32, 66), BF),
            jax.ShapeDtypeStruct((4, PY, 256, 128), BF),
        ),
        in_specs=[any_spec, vmem, any_spec, any_spec] + [vmem] * 9,
        out_specs=(any_spec, any_spec),
        scratch_shapes=[
            pltpu.VMEM((4 * PY, 256, 128), F32),
            pltpu.VMEM((32, 32, 32, 66), BF),
            pltpu.VMEM((2, 2048, 1024), BF),
            pltpu.VMEM((2 * PY, KZ, 16, 128), BF),
            pltpu.VMEM((2 * PY, KZ, 16, 128), BF),
            pltpu.VMEM((2 * PX, KZ, 16, 128), BF),
            pltpu.VMEM((2 * PX, KZ, 16, 128), BF),
            pltpu.VMEM((PX, 2, MR, 128), BF),
            pltpu.VMEM((PY, MR, 128), BF),
            pltpu.VMEM((PY, MR, 128), BF),
            pltpu.VMEM((PX, 2, MR, 128), BF),
            pltpu.VMEM((CR, 2048), BF),
            pltpu.VMEM((CR, 1024), BF),
            pltpu.VMEM((4096, 128), F32),
            pltpu.VMEM((4096, 128), F32),
            pltpu.VMEM((576, 128), F32),
            pltpu.VMEM((1024, 128), F32),
            pltpu.VMEM((PY, 4, 256, 128), BF),
            dma((PY,)), dma, dma, dma((32,)), dma((PY,)), dma,
            dma((PY,)), dma((PY,)), dma((PX,)), dma((PX,)), dma((PX, 2)), dma((PY,)),
            dma((PY,)), dma((PX, 2)), dma((PX,)), dma((PX,)), dma((PY,)), dma((PY,)),
        ],
        compiler_params=pltpu.CompilerParams(
            collective_id=0, has_side_effects=True, vmem_limit_bytes=54 * 1024 * 1024
        ),
    )(og, xm, w, xf, zf, zi, yf, yi, perm, permt, place, back, dup)
    return wg.reshape(32, 32, 8, 4, 66), ig.reshape(4, 32, 16, 8, 128)


def solution(mesh):
    spec = P(None, None, "px", "py", None)
    return jax.shard_map(
        body, mesh=mesh, in_specs=(spec, spec, spec), out_specs=(spec, spec), check_vma=False
    )
```

time: 705 us -> 178 us (0.25)
  the two profiles are of different devices: /device:TPU:22 before, /device:TPU:9 now
where the time goes in v1:
time: 178 us
  Pallas kernels  166 us (93%)
  local copies, waits for them, and re-layouts  10.8 us (6%)
    pallas_call x1, Pallas kernels, body(): pl.pallas_call(kernel, out_shape=(jax.ShapeDtypeStruct((32, 32, 32, 66),...  166 us
    unnamed x4, local copies, waits for them, and re-layouts  10.8 us

profile of v1, /device:TPU:9, one launch (start us, length us, event | category | flops | bytes accessed | tf_op | source)
XLA Modules:
  0.0 178.0 jit_solution(8885643713089158623)
XLA Ops:
  0.6 166.5 %shard_map.140 = (bf16[32,32,32,66]{3,2,1,0:T(8,128)(2,1)}, bf16[4,16,256,128]{3,2,1,0:T(8,128)(2,1)}) custom-call(f32[4,16,256,128]{3,2,1,0:T(8,128)} %bitcast.5, bf16[4096,66]{1,0:T(8,128)(2,1)} %bitcast.9, bf16[32,32,32,66]{3,2,1,0:T(8,128)(2,1)} %bitcast.6, bf16[2,2048,1024]{2,1,0:T(8,128)(2,1)} %constant.24.clone.xf_hbm, ...), custom_call_target="tpu_custom_call" | custom-call | tf_op jit(solution)/shard_map/pallas_call | solution.py:532
  167.1 0.0 copy-start
  167.1 8.8 %copy.17 = bf16[32,32,8,4,66]{4,3,2,1,0:T(4,128)(2,1)} copy(bf16[32,32,8,4,66]{4,3,2,1,0:T(4,128)(2,1)} %bitcast.7) | data formatting | bytes 8650752
  175.9 0.0 copy-done
  175.9 2.0 %copy.18 = bf16[4,32,16,8,128]{4,3,2,1,0:T(8,128)(2,1)} copy(bf16[4,32,16,8,128]{4,3,2,1,0:T(8,128)(2,1)S(1)} %bitcast.8) | data formatting | bytes 8388608
Async XLA Ops:
  167.1 8.8 %copy-start = (bf16[4,16,256,128]{3,2,1,0:T(8,128)(2,1)S(1)}, bf16[4,16,256,128]{3,2,1,0:T(8,128)(2,1)}, u32[]{:S(2)}) copy-start(bf16[4,16,256,128]{3,2,1,0:T(8,128)(2,1)} %get-tuple-element.5) | copy-start | bytes 12582916

commit v2 on v1

--- a/solution.py
+++ b/solution.py
@@ -18,6 +18,7 @@
 PX = 8
 PY = 16
 MR = 144
+KG = 11
 CR = 272
 T1, T2, G, GS = 0, 16, 32, 48
 
@@ -110,11 +111,11 @@
 def kernel(
     og, xm, w_hbm, xf_hbm, zf, zi, yf, yi, perm, permt, place, back, dup,
     wg, ig,
-    ogv, wv, xfv, send_a, recv_a, send_b, recv_b, send_m, recv_m, send_n, recv_n,
+    ogv, wv, xfv, send_a, recv_a, send_b, recv_b, send_m, recv_m, send_n, pass_n, recv_n,
     lines, dm, xr, xi, blk, turn, outv,
     og_sem, w_sem, xf_sem, wg_sem, ig_sem, self_sem,
     sa_sem, ra_sem, sb_sem, rb_sem, sm_sem, rm_sem,
-    sn_sem, rn_sem, sc_sem, rc_sem, sd_sem, rd_sem,
+    sn_sem, rn_sem, sp_sem, rp_sem, sc_sem, rc_sem, sd_sem, rd_sem,
 ):
     px = lax.axis_index("px")
     py = lax.axis_index("py")
@@ -165,16 +166,18 @@
             src_ref=send_a.at[src], dst_ref=recv_a.at[src], send_sem=sa_sem.at[src], recv_sem=ra_sem.at[src],
             device_id=(px, src), device_id_type=MESH)
 
-    def copy_b(s):
+    def copy_b(s, part):
         to = lax.rem(px + s, PX)
-        return pltpu.make_async_remote_copy(
-            src_ref=send_b.at[to], dst_ref=recv_b.at[px], send_sem=sb_sem.at[to], recv_sem=rb_sem.at[px],
-            device_id=(to, py), device_id_type=MESH)
-
-    def arrive_b(src):
-        return pltpu.make_async_remote_copy(
-            src_ref=send_b.at[src], dst_ref=recv_b.at[src], send_sem=sb_sem.at[src], recv_sem=rb_sem.at[src],
-            device_id=(src, py), device_id_type=MESH)
+        ks = pl.ds(part * KG, KG)
+        return pltpu.make_async_remote_copy(
+            src_ref=send_b.at[to, ks], dst_ref=recv_b.at[px, ks], send_sem=sb_sem.at[part, to],
+            recv_sem=rb_sem.at[part, px], device_id=(to, py), device_id_type=MESH)
+
+    def arrive_b(src, part):
+        ks = pl.ds(part * KG, KG)
+        return pltpu.make_async_remote_copy(
+            src_ref=send_b.at[src, ks], dst_ref=recv_b.at[src, ks], send_sem=sb_sem.at[part, src],
+            recv_sem=rb_sem.at[part, src], device_id=(src, py), device_id_type=MESH)
 
     def copy_m(to_x, h):
         return pltpu.make_async_remote_copy(
@@ -182,10 +185,24 @@
             device_id=(to_x, 2 * px + h), device_id_type=MESH)
 
     def copy_n(to_y):
-        h = lax.rem(py, 2)
-        return pltpu.make_async_remote_copy(
-            src_ref=send_n.at[to_y], dst_ref=recv_n.at[px, h], send_sem=sn_sem.at[to_y], recv_sem=rn_sem.at[px, h],
-            device_id=(owner_px, to_y), device_id_type=MESH)
+        return pltpu.make_async_remote_copy(
+            src_ref=send_n.at[to_y], dst_ref=pass_n.at[py], send_sem=sn_sem.at[to_y], recv_sem=rn_sem.at[py],
+            device_id=(px, to_y), device_id_type=MESH)
+
+    def arrive_n(src):
+        return pltpu.make_async_remote_copy(
+            src_ref=send_n.at[src], dst_ref=pass_n.at[src], send_sem=sn_sem.at[src], recv_sem=rn_sem.at[src],
+            device_id=(px, src), device_id_type=MESH)
+
+    def copy_p(to):
+        return pltpu.make_async_remote_copy(
+            src_ref=pass_n.at[pl.ds(2 * to, 2)], dst_ref=recv_n.at[px], send_sem=sp_sem.at[to],
+            recv_sem=rp_sem.at[px], device_id=(to, py), device_id_type=MESH)
+
+    def arrive_p(src):
+        return pltpu.make_async_remote_copy(
+            src_ref=pass_n.at[pl.ds(2 * src, 2)], dst_ref=recv_n.at[src], send_sem=sp_sem.at[src],
+            recv_sem=rp_sem.at[src], device_id=(src, py), device_id_type=MESH)
 
     def copy_c(s):
         to = lax.rem(px + s, PX)
@@ -198,16 +215,18 @@
             src_ref=send_b.at[PX + src], dst_ref=recv_b.at[PX + src], send_sem=sc_sem.at[src], recv_sem=rc_sem.at[src],
             device_id=(src, py), device_id_type=MESH)
 
-    def copy_d(s):
+    def copy_d(s, part):
         to = lax.rem(py + s, PY)
-        return pltpu.make_async_remote_copy(
-            src_ref=send_a.at[PY + to], dst_ref=recv_a.at[PY + py], send_sem=sd_sem.at[to], recv_sem=rd_sem.at[py],
-            device_id=(px, to), device_id_type=MESH)
-
-    def arrive_d(src):
-        return pltpu.make_async_remote_copy(
-            src_ref=send_a.at[PY + src], dst_ref=recv_a.at[PY + src], send_sem=sd_sem.at[src], recv_sem=rd_sem.at[src],
-            device_id=(px, src), device_id_type=MESH)
+        ks = pl.ds(part * KG, KG)
+        return pltpu.make_async_remote_copy(
+            src_ref=send_a.at[PY + to, ks], dst_ref=recv_a.at[PY + py, ks], send_sem=sd_sem.at[part, to],
+            recv_sem=rd_sem.at[part, py], device_id=(px, to), device_id_type=MESH)
+
+    def arrive_d(src, part):
+        ks = pl.ds(part * KG, KG)
+        return pltpu.make_async_remote_copy(
+            src_ref=send_a.at[PY + src, ks], dst_ref=recv_a.at[PY + src, ks], send_sem=sd_sem.at[part, src],
+            recv_sem=rd_sem.at[part, src], device_id=(px, src), device_id_type=MESH)
 
     def z_forward(chunk):
         pltpu.make_async_copy(og.at[:, chunk], ogv.at[pl.ds(chunk * 4, 4)], og_sem.at[chunk]).wait()
@@ -264,13 +283,16 @@
         send_b[0:PX, k] = res.reshape(PX, 16, 128)
         return c
 
-    lax.fori_loop(0, KZ, step_b, 0, unroll=3)
-
-    def start_b(s, c):
-        copy_b(s).start()
-        return c
-
-    lax.fori_loop(1, PX, start_b, 0)
+    def part_b(part, c):
+        lax.fori_loop(part * KG, part * KG + KG, step_b, 0, unroll=True)
+
+        def start_b(s, c2):
+            copy_b(s, part).start()
+            return c2
+
+        return lax.fori_loop(1, PX, start_b, c)
+
+    lax.fori_loop(0, 3, part_b, 0)
     pltpu.make_async_copy(xf_hbm, xfv, xf_sem).wait()
 
     def gather_b(src, data):
@@ -281,7 +303,8 @@
 
     def step_gather(s, c):
         src = lax.rem(px + PX - s, PX)
-        arrive_b(src).wait_recv()
+        for part in range(3):
+            arrive_b(src, part).wait_recv()
         gather_b(src, recv_b[src])
         return c
 
@@ -289,71 +312,82 @@
     lax.fori_loop(1, PX, step_gather, 0)
 
     def step_c(k, c):
-        cols = pl.ds(pl.multiple_of(k * 256, 256), 256)
+        pair = lax.rem(px // 2 + py + k, 4)
+        cols = pl.ds(pl.multiple_of(pair * 256, 256), 256)
         res = dot(lines[...], xfv[0, :, cols]) + dot(lines[...], xfv[1, :, cols])
         moved = dot(perm[...], res.astype(BF)).astype(BF)
         for e in range(2):
-            send_m[2 * k + e] = moved[:, e * 128:(e + 1) * 128].reshape(2, MR, 128)
+            send_m[2 * pair + e] = moved[:, e * 128:(e + 1) * 128].reshape(2, MR, 128)
         for e in range(2):
             for h in range(2):
-                own = jnp.logical_and(2 * k + e == px, 2 * px + h == py)
+                own = jnp.logical_and(2 * pair + e == px, 2 * px + h == py)
 
                 @pl.when(jnp.logical_not(own))
                 def _():
-                    copy_m(2 * k + e, h).start()
+                    copy_m(2 * pair + e, h).start()
 
                 @pl.when(own)
                 def _():
-                    local = pltpu.make_async_copy(send_m.at[2 * k + e, h], recv_m.at[py], self_sem)
+                    local = pltpu.make_async_copy(send_m.at[2 * pair + e, h], recv_m.at[py], self_sem)
                     local.start()
                     local.wait()
         return c
 
     lax.fori_loop(0, 4, step_c, 0)
 
-    def step_place(src, c):
-        @pl.when(jnp.logical_not(jnp.logical_and(owner_px == px, src == py)))
-        def _():
-            pltpu.make_async_remote_copy(
-                src_ref=send_m.at[0, 0], dst_ref=recv_m.at[src], send_sem=sm_sem.at[0, 0], recv_sem=rm_sem.at[src],
-                device_id=(owner_px, src), device_id_type=MESH).wait_recv()
-
-        turned = recv_m[src].astype(F32).T.astype(BF)
-        res = dot(turned[0:64], place[0]) + dot(turned[64:128], place[1])
+    def senders(k):
+        first = lax.rem(px // 2 + 8 - owner_px // 2 - k, 4)
+        return [first + 4 * m for m in range(4)]
+
+    def place_modes(k):
+        real, imag = [], []
+        for src in senders(k):
+            @pl.when(jnp.logical_not(jnp.logical_and(owner_px == px, src == py)))
+            def _():
+                pltpu.make_async_remote_copy(
+                    src_ref=send_m.at[0, 0], dst_ref=recv_m.at[src], send_sem=sm_sem.at[0, 0], recv_sem=rm_sem.at[src],
+                    device_id=(owner_px, src), device_id_type=MESH).wait_recv()
+
+            turned = recv_m[src].astype(F32).T.astype(BF)
+            real.append(turned[0:64])
+            imag.append(turned[64:128])
+        real, imag = jnp.concatenate(real, axis=0), jnp.concatenate(imag, axis=0)
         for r in range(4):
-            rows = pl.ds(r, 64, stride=4)
-            ogv[G + src, rows, :] = res[:, r * 256:r * 256 + 128]
-            ogv[GS + src, rows, :] = res[:, r * 256 + 128:r * 256 + 256]
-        return c
-
-    lax.fori_loop(0, PY, step_place, 0)
+            cols = slice(r * 256, r * 256 + 256)
+            res = dot(real, place[0, :, cols]) + dot(imag, place[1, :, cols])
+            for m, src in enumerate(senders(k)):
+                rows = pl.ds(r, 64, stride=4)
+                ogv[G + src, rows, :] = res[m * 64:m * 64 + 64, 0:128]
+                ogv[GS + src, rows, :] = res[m * 64:m * 64 + 64, 128:256]
+
     pltpu.make_async_copy(w_hbm, wv, w_sem).wait()
 
-    def step_modes(k, c):
-        pair, half = k // 2, lax.rem(k, 2)
-        off = pl.multiple_of(half * 16, 16)
-
-        def add(op, acc):
-            acc = list(acc)
+    def step_modes(pair, off, k):
+        tv, uv = ogv.at[T1 + pair], ogv.at[T2 + pair]
+        acc = []
+        for ii in range(2):
+            for b in range(4):
+                at = (b * 2 + ii) * 32 + off
+                acc.append(tv[at:at + 16, 0:66])
+                acc.append(uv[at:at + 16, 0:66])
+        for src in senders(k):
+            gv, sv = ogv.at[G + src], ogv.at[GS + src]
+            wp = [wv.at[2 * pair + ii, pl.ds(2 * src, 2)] for ii in range(2)]
             for oo in range(2):
-                w = [wv[2 * pair + ii, 2 * op + oo, pl.ds(off, 16), :].astype(F32) for ii in range(2)]
+                w = [wp[ii][oo, off:off + 16, :].astype(F32) for ii in range(2)]
                 for b in range(4):
-                    rows = pl.ds(pl.multiple_of((b * 2 + oo) * 32 + off, 16), 16)
-                    gb = ogv[G + op, rows, 0:66]
-                    sb = ogv[GS + op, rows, 0:66]
+                    at = (b * 2 + oo) * 32 + off
+                    gb = gv[at:at + 16, 0:66]
+                    sb = sv[at:at + 16, 0:66]
                     for ii in range(2):
                         n = (ii * 4 + b) * 2
                         acc[n] = acc[n] + w[ii] * gb
                         acc[n + 1] = acc[n + 1] + w[ii] * sb
-            return tuple(acc)
-
-        acc = lax.fori_loop(0, 16, add, tuple(jnp.zeros((16, 66), F32) for _ in range(16)))
         for ii in range(2):
             for b in range(4):
-                rows = pl.ds(pl.multiple_of((b * 2 + ii) * 32 + off, 16), 16)
-                ogv[T1 + pair, rows, 0:66] = acc[(ii * 4 + b) * 2]
-                ogv[T2 + pair, rows, 0:66] = acc[(ii * 4 + b) * 2 + 1]
-        return c
+                at = (b * 2 + ii) * 32 + off
+                tv[at:at + 16, 0:66] = acc[(ii * 4 + b) * 2]
+                uv[at:at + 16, 0:66] = acc[(ii * 4 + b) * 2 + 1]
 
     def step_return(k, c):
         def rows_of(base, r):
@@ -365,63 +399,94 @@
             both = jnp.concatenate([rows_of(T1, r), rows_of(T2, r)], axis=0).astype(BF)
             total = total + dot_nt(back[:, r * 128:(r + 1) * 128], both)
         send_n[k] = total.astype(BF)
-        own = jnp.logical_and(owner_px == px, k == py)
-
-        @pl.when(jnp.logical_not(own))
+
+        @pl.when(k != py)
         def _():
             copy_n(k).start()
 
-        @pl.when(own)
-        def _():
-            local = pltpu.make_async_copy(send_n.at[k], recv_n.at[px, lax.rem(py, 2)], self_sem)
+        @pl.when(k == py)
+        def _():
+            local = pltpu.make_async_copy(send_n.at[k], pass_n.at[py], self_sem)
             local.start()
             local.wait()
 
         return c
 
-    def step_pair(k, c):
-        step_modes(2 * k, 0)
-        step_modes(2 * k + 1, 0)
-        return step_return(k, c)
-
-    lax.fori_loop(0, 16, step_pair, 0)
-
-    def step_weight(k, c):
-        i, half = k // 2, lax.rem(k, 2)
-        off = pl.multiple_of(half * 16, 16)
-        xrb = [xr[pl.ds(pl.multiple_of((b * 32 + i) * 32 + off, 16), 16), 0:66] for b in range(4)]
-        xib = [xi[pl.ds(pl.multiple_of((b * 32 + i) * 32 + off, 16), 16), 0:66] for b in range(4)]
-
-        def one(op, c2):
-            for oo in range(2):
-                total = None
-                for b in range(4):
-                    rows = pl.ds(pl.multiple_of((b * 2 + oo) * 32 + off, 16), 16)
-                    term = xrb[b] * ogv[G + op, rows, 0:66] + xib[b] * ogv[GS + op, rows, 0:66]
-                    total = term if total is None else total + term
-                wv[i, 2 * op + oo, pl.ds(off, 16), :] = total.astype(BF)
+    def step_group(k, c):
+        place_modes(k)
+
+        def step_pair(pair, c2):
+            step_modes(pair, 0, k)
+            step_modes(pair, 16, k)
             return c2
 
-        lax.fori_loop(0, 16, one, 0)
-
-        @pl.when(half == 1)
-        def _():
-            pltpu.make_async_copy(wv.at[i], wg.at[i], wg_sem.at[i]).start()
-
-        return c
-
-    lax.fori_loop(0, 22, step_weight, 0)
-
-    def step_unplace(k, c):
+        return lax.fori_loop(0, 16, step_pair, c)
+
+    lax.fori_loop(0, 3, step_group, 0)
+    place_modes(3)
+
+    def step_last(s, c):
+        pair = lax.rem(py + s, PY)
+        step_modes(pair, 0, 3)
+        step_modes(pair, 16, 3)
+        return step_return(pair, c)
+
+    lax.fori_loop(0, 16, step_last, 0)
+
+    def step_weight(i, c):
+        for off in (0, 16):
+            xrb = [xr[pl.ds(pl.multiple_of((b * 32 + i) * 32 + off, 16), 16), 0:66] for b in range(4)]
+            xib = [xi[pl.ds(pl.multiple_of((b * 32 + i) * 32 + off, 16), 16), 0:66] for b in range(4)]
+
+            def one(op, c2):
+                gv, sv, out = ogv.at[G + op], ogv.at[GS + op], wv.at[i, pl.ds(2 * op, 2)]
+                for oo in range(2):
+                    total = None
+                    for b in range(4):
+                        at = (b * 2 + oo) * 32 + off
+                        term = xrb[b] * gv[at:at + 16, 0:66] + xib[b] * sv[at:at + 16, 0:66]
+                        total = term if total is None else total + term
+                    out[oo, off:off + 16, :] = total.astype(BF)
+                return c2
+
+            lax.fori_loop(0, 16, one, 0)
+
+        pltpu.make_async_copy(wv.at[i], wg.at[i], wg_sem.at[i]).start()
+        return c
+
+    lax.fori_loop(0, 6, step_weight, 0)
+
+    def step_pass(s, c):
+        to = lax.rem(px + s, PX)
         for h in range(2):
-            @pl.when(jnp.logical_not(jnp.logical_and(k == px, 2 * px + h == py)))
+            @pl.when(2 * to + h != py)
             def _():
-                pltpu.make_async_remote_copy(
-                    src_ref=send_n.at[0], dst_ref=recv_n.at[k, h], send_sem=sn_sem.at[0], recv_sem=rn_sem.at[k, h],
-                    device_id=(k, 2 * px + h), device_id_type=MESH).wait_recv()
-
-        moved = dot(permt[...], recv_n[k].reshape(2 * MR, 128))
-        dm[:, pl.ds(pl.multiple_of(k * 128, 128), 128)] = moved.astype(BF)
+                arrive_n(2 * to + h).wait_recv()
+
+        @pl.when(s != PX)
+        def _():
+            copy_p(to).start()
+
+        @pl.when(s == PX)
+        def _():
+            local = pltpu.make_async_copy(pass_n.at[pl.ds(2 * to, 2)], recv_n.at[px], self_sem)
+            local.start()
+            local.wait()
+
+        return c
+
+    lax.fori_loop(1, PX + 1, step_pass, 0)
+    lax.fori_loop(6, 13, step_weight, 0)
+
+    def step_unplace(s, c):
+        src = lax.rem(px + PX - s, PX)
+
+        @pl.when(s != 0)
+        def _():
+            arrive_p(src).wait_recv()
+
+        moved = dot(permt[...], recv_n[src].reshape(2 * MR, 128))
+        dm[:, pl.ds(pl.multiple_of(src * 128, 128), 128)] = moved.astype(BF)
         return c
 
     lax.fori_loop(0, PX, step_unplace, 0)
@@ -443,7 +508,7 @@
     lax.fori_loop(1, PX, step_cb, 0)
     recv_b[PX + px] = x_inverse(px)
 
-    lax.fori_loop(22, 44, step_weight, 0)
+    lax.fori_loop(13, 24, step_weight, 0)
 
     def wait_c(s, c):
         arrive_c(lax.rem(px + PX - s, PX)).wait_recv()
@@ -457,14 +522,17 @@
         send_a[PY:2 * PY, k] = res.reshape(PY, 16, 128)
         return c
 
-    lax.fori_loop(0, KZ, step_bb, 0, unroll=3)
-
-    def start_d(s, c):
-        copy_d(s).start()
-        return c
-
-    lax.fori_loop(1, PY, start_d, 0)
-    lax.fori_loop(44, 64, step_weight, 0)
+    def part_d(part, c):
+        lax.fori_loop(part * KG, part * KG + KG, step_bb, 0, unroll=True)
+
+        def start_d(s, c2):
+            copy_d(s, part).start()
+            return c2
+
+        return lax.fori_loop(1, PY, start_d, c)
+
+    lax.fori_loop(0, 3, part_d, 0)
+    lax.fori_loop(24, 32, step_weight, 0)
 
     blk[528:576, :] = jnp.zeros((48, 128), F32)
 
@@ -481,20 +549,25 @@
 
     def step_d(s, c):
         src = lax.rem(py + PY - s, PY)
-        arrive_d(src).wait_recv()
+        for part in range(3):
+            arrive_d(src, part).wait_recv()
         z_inverse(src, recv_a[PY + src])
         return c
 
     lax.fori_loop(1, PY, step_d, 0)
 
     def end_px(s, c):
-        copy_b(s).wait_send()
+        for part in range(3):
+            copy_b(s, part).wait_send()
         copy_c(s).wait_send()
+        copy_p(lax.rem(px + s, PX)).wait_send()
         return c
 
     def end_py(s, c):
         copy_a(s).wait_send()
-        copy_d(s).wait_send()
+        for part in range(3):
+            copy_d(s, part).wait_send()
+        copy_n(lax.rem(py + s, PY)).wait_send()
         return c
 
     def end_m(t, c):
@@ -503,10 +576,6 @@
         @pl.when(jnp.logical_not(jnp.logical_and(to_x == px, 2 * px + h == py)))
         def _():
             copy_m(to_x, h).wait_send()
-
-        @pl.when(jnp.logical_not(jnp.logical_and(owner_px == px, t == py)))
-        def _():
-            copy_n(t).wait_send()
 
         pltpu.make_async_copy(outv.at[t], ig.at[:, t], ig_sem.at[t]).wait()
         return c
@@ -519,6 +588,22 @@
     lax.fori_loop(1, PY, end_py, 0)
     lax.fori_loop(0, PY, end_m, 0)
     lax.fori_loop(0, 32, end_w, 0)
+
+
+def hand_on(held, wg, buf, in_sem, out_sem):
+    def load(i):
+        return pltpu.make_async_copy(held.at[pl.ds(2 * i, 2)], buf.at[pl.ds(2 * i, 2)], in_sem.at[i])
+
+    def store(i):
+        return pltpu.make_async_copy(buf.at[pl.ds(2 * i, 2)], wg.at[pl.ds(2 * i, 2)], out_sem.at[i])
+
+    for i in range(16):
+        load(i).start()
+    for i in range(16):
+        load(i).wait()
+        store(i).start()
+    for i in range(16):
+        store(i).wait()
 
 
 def body(out_grad, input_modes, mode_weights):
@@ -548,6 +633,7 @@
             pltpu.VMEM((PX, 2, MR, 128), BF),
             pltpu.VMEM((PY, MR, 128), BF),
             pltpu.VMEM((PY, MR, 128), BF),
+            pltpu.VMEM((PY, MR, 128), BF),
             pltpu.VMEM((PX, 2, MR, 128), BF),
             pltpu.VMEM((CR, 2048), BF),
             pltpu.VMEM((CR, 1024), BF),
@@ -557,13 +643,22 @@
             pltpu.VMEM((1024, 128), F32),
             pltpu.VMEM((PY, 4, 256, 128), BF),
             dma((PY,)), dma, dma, dma((32,)), dma((PY,)), dma,
-            dma((PY,)), dma((PY,)), dma((PX,)), dma((PX,)), dma((PX, 2)), dma((PY,)),
-            dma((PY,)), dma((PX, 2)), dma((PX,)), dma((PX,)), dma((PY,)), dma((PY,)),
+            dma((PY,)), dma((PY,)), dma((3, PX)), dma((3, PX)), dma((PX, 2)), dma((PY,)),
+            dma((PY,)), dma((PY,)), dma((PX,)), dma((PX,)), dma((PX,)), dma((PX,)), dma((3, PY)), dma((3, PY)),
         ],
         compiler_params=pltpu.CompilerParams(
             collective_id=0, has_side_effects=True, vmem_limit_bytes=54 * 1024 * 1024
         ),
     )(og, xm, w, xf, zf, zi, yf, yi, perm, permt, place, back, dup)
+    wg = pl.pallas_call(
+        hand_on,
+        out_shape=jax.ShapeDtypeStruct((32, 32, 32, 66), BF),
+        in_specs=[any_spec],
+        out_specs=any_spec,
+        scratch_shapes=[pltpu.VMEM((32, 32, 32, 66), BF), dma((16,)), dma((16,))],
+        compiler_params=pltpu.CompilerParams(vmem_limit_bytes=54 * 1024 * 1024),
+        cost_estimate=pl.CostEstimate(flops=0, bytes_accessed=17000000, transcendentals=0),
+    )(wg)
     return wg.reshape(32, 32, 8, 4, 66), ig.reshape(4, 32, 16, 8, 128)
 
 

time: 178 us -> 157 us (0.88); the launches traced: 178 us -> 154 us
  Pallas kernels: 166 us -> 151 us
  local copies, waits for them, and re-layouts: 10.8 us -> 2.85 us
    pallas_call x1, Pallas kernels: 166 us -> 144 us  [body(): pl.pallas_call(kernel, out_shape=(jax.ShapeDtypeStruct((32, 32, 32, 66),...]
    unnamed x4 -> x3, local copies, waits for them, and re-layouts: 10.8 us -> 2.85 us
    pallas_call x0 -> x1, Pallas kernels: none -> 6.72 us  [body(): pl.pallas_call(hand_on, out_shape=jax.ShapeDtypeStruct((32, 32, 32, 66),...]
where the time goes in v2:
time: 157 us; the launch traced here: 154 us
  Pallas kernels  151 us (96%)
  local copies, waits for them, and re-layouts  2.85 us (2%)
    pallas_call x1, Pallas kernels, body(): pl.pallas_call(kernel, out_shape=(jax.ShapeDtypeStruct((32, 32, 32, 66),...  144 us
    pallas_call x1, Pallas kernels, body(): pl.pallas_call(hand_on, out_shape=jax.ShapeDtypeStruct((32, 32, 32, 66),...  6.72 us

profile of v2, /device:TPU:9, one launch (start us, length us, event | category | flops | bytes accessed | tf_op | source)
XLA Modules:
  0.0 154.2 jit_solution(11729863505917252212)
XLA Ops:
  0.6 144.0 %shard_map.140 = (bf16[32,32,32,66]{3,2,1,0:T(8,128)(2,1)}, bf16[4,16,256,128]{3,2,1,0:T(8,128)(2,1)}) custom-call(f32[4,16,256,128]{3,2,1,0:T(8,128)} %bitcast.5, bf16[4096,66]{1,0:T(8,128)(2,1)} %bitcast.9, bf16[32,32,32,66]{3,2,1,0:T(8,128)(2,1)} %bitcast.6, bf16[2,2048,1024]{2,1,0:T(8,128)(2,1)} %constant.24.clone.xf_hbm, ...), custom_call_target="tpu_custom_call" | custom-call | tf_op jit(solution)/shard_map/pallas_call | solution.py:617
  144.6 0.0 copy-start
  144.6 6.7 %shard_map.141 = bf16[32,32,32,66]{3,2,1,0:T(8,128)(2,1)} custom-call(bf16[32,32,32,66]{3,2,1,0:T(8,128)(2,1)} %get-tuple-element.4.held), custom_call_target="tpu_custom_call" | custom-call | bytes 17000000 | tf_op jit(solution)/shard_map/pallas_call | solution.py:653
  151.4 0.8 copy-done
  152.2 2.0 %copy.16 = bf16[4,32,16,8,128]{4,3,2,1,0:T(8,128)(2,1)} copy(bf16[4,32,16,8,128]{4,3,2,1,0:T(8,128)(2,1)S(1)} %bitcast.8) | data formatting | bytes 8388608
Async XLA Ops:
  144.6 7.6 %copy-start = (bf16[4,16,256,128]{3,2,1,0:T(8,128)(2,1)S(1)}, bf16[4,16,256,128]{3,2,1,0:T(8,128)(2,1)}, u32[]{:S(2)}) copy-start(bf16[4,16,256,128]{3,2,1,0:T(8,128)(2,1)} %get-tuple-element.5) | copy-start | bytes 12582916

commit v3 on v2

v3 whole, which is shorter than its diff:
```python
import math

import jax
import jax.numpy as jnp
import ml_dtypes
import numpy as np
from jax import lax
from jax.experimental import pallas as pl
from jax.experimental.pallas import tpu as pltpu
from jax.sharding import PartitionSpec as P

BF = jnp.bfloat16
F32 = jnp.float32
MESH = pl.DeviceIdType.MESH
N = 128
KEPT = 64
KZ = 33
PX = 8
PY = 16
MR = 144
W1, W2 = 7, 20
KG = 11
NR = 48
CR = 272
T1, T2, G, GS = 0, 16, 32, 48


def split(table):
    high = table.astype(ml_dtypes.bfloat16)
    low = (table - high.astype(np.float64)).astype(ml_dtypes.bfloat16)
    return high, low


def tables():
    bf = ml_dtypes.bfloat16
    grid = np.arange(N)
    angle_z = 2 * math.pi * (np.outer(np.arange(KZ), grid) % N) / N
    norm = 1.0 / math.sqrt(N)
    cz, sz = np.cos(angle_z) * norm, np.sin(angle_z) * norm
    kept = np.concatenate([np.arange(KEPT // 2), np.arange(N - KEPT // 2, N)])
    angle = 2 * math.pi * (np.outer(kept, grid) % N) / N
    cos, sin = np.cos(angle) * norm, np.sin(angle) * norm

    fz = np.stack([cz, -sz], axis=1).reshape(2 * KZ, N)
    hi, lo = split(fz)
    zf = np.zeros((144, 256), bf)
    zf[:66, :128] = hi
    zf[:66, 128:] = hi
    zf[72:138, :128] = lo
    weight = np.where(np.arange(KZ) == 0, 1.0, 2.0)[:, None]
    iz = np.stack([weight * cz, -weight * sz], axis=1).reshape(2 * KZ, N)
    hi, lo = split(iz)
    zi = np.zeros((2, 72, N), bf)
    zi[0, :66] = hi
    zi[1, :66] = lo

    full = np.zeros((2, KEPT, 2, N))
    full[0, :, 0] = cos
    full[0, :, 1] = sin
    full[1, :, 0] = -sin
    full[1, :, 1] = cos

    wy = full.reshape(2, PX, 8, 2, PY, 8).transpose(1, 0, 2, 4, 3, 5).reshape(128, 256)
    hi, lo = split(wy)
    yf = np.concatenate([hi, lo], axis=0)
    held = 4 * (2 * np.arange(8)[None, :] + np.arange(PX)[:, None] // 4) + np.arange(PX)[:, None] % 4
    wy = full[:, held.reshape(-1)].reshape(2, PX, 8, 2, PY, 8).transpose(1, 0, 2, 4, 3, 5).reshape(128, 256)
    hi, lo = split(wy)
    yi = np.concatenate([hi.T, lo.T], axis=1)

    wx = full.reshape(2, PX, 8, 2, PX, 16).transpose(4, 3, 5, 1, 0, 2)
    hi, lo = split(wx)
    xf = np.zeros((2, PX, 2, 8, 16, PX, 2, 8, 8), bf)
    for bc in range(8):
        xf[0, :, :, bc, :, :, :, bc, :] = hi
        xf[1, :, :, bc, :, :, :, bc, :] = lo
    xf = xf.reshape(2, 2048, 1024)

    perm = np.zeros((2, MR, CR), bf)
    for h in range(2):
        for k in range(KZ):
            for r in range(4):
                perm[h, 4 * k + r, 8 * k + 4 * h + r] = 1
    perm = perm.reshape(2 * MR, CR)
    permt = np.zeros((CR, 8, NR), bf)
    for t in range(8):
        for k in range(KZ):
            permt[8 * k + t, t, k] = 1
    permt = permt.reshape(CR, 8 * NR)

    place = np.zeros((2, MR, 4, 2, 128), bf)
    back = np.zeros((NR, 128), bf)
    for k in range(KZ):
        for r in range(4):
            place[0, 4 * k + r, r, 0, k] = 1
            place[1, 4 * k + r, r, 0, KZ + k] = 1
            place[1, 4 * k + r, r, 1, k] = 1
            place[0, 4 * k + r, r, 1, KZ + k] = -1
    place = place.reshape(2, MR, 1024)
    back[np.arange(KZ), np.arange(KZ)] = 1

    dup = np.zeros((2 * KZ, 2, 128), bf)
    for k in range(KZ):
        for part in range(2):
            dup[part * KZ + k, part, k] = 1
            dup[part * KZ + k, part, KZ + k] = 1
    dup = dup.reshape(2 * KZ, 256)
    return zf, zi, yf, yi, xf, perm, permt, place, back, dup


def dot(a, b):
    return jnp.dot(a, b, preferred_element_type=F32)


def dot_nt(a, b):
    return lax.dot_general(a, b, (((1,), (1,)), ((), ())), preferred_element_type=F32)


def kernel(
    og, xm, w_hbm, xf_hbm, zf, yf, yi, perm, permt, place, back, dup,
    wg, lines_out,
    ogv, wv, xfv, send_a, recv_a, send_b, recv_b, send_m, recv_m, send_n, recv_n,
    lines, sums, dm, xr, xi, blk,
    og_sem, w_sem, xf_sem, wg_sem, self_sem,
    sa_sem, ra_sem, sb_sem, rb_sem, sm_sem, rm_sem,
    sn_sem, rn_sem, sc_sem, rc_sem, sd_sem, rd_sem,
):
    px = lax.axis_index("px")
    py = lax.axis_index("py")
    owner_px = py // 2

    for k in range(PY):
        chunk = lax.rem(py + 1 + k, PY)
        pltpu.make_async_copy(og.at[:, chunk], ogv.at[pl.ds(chunk * 4, 4)], og_sem.at[chunk]).start()
    pltpu.make_async_copy(xf_hbm, xfv, xf_sem).start()
    pltpu.make_async_copy(w_hbm, wv, w_sem).start()

    barrier = pltpu.get_barrier_semaphore()
    me = px * PY + py

    def greet(k, c):
        to = lax.rem(me + k, PX * PY)
        pl.semaphore_signal(barrier, inc=1, device_id=(to // PY, lax.rem(to, PY)), device_id_type=MESH)
        return c

    lax.fori_loop(1, PX * PY, greet, 0)

    def copy_a(s):
        to = lax.rem(py + s, PY)
        return pltpu.make_async_remote_copy(
            src_ref=send_a.at[to], dst_ref=recv_a.at[py], send_sem=sa_sem.at[to], recv_sem=ra_sem.at[py],
            device_id=(px, to), device_id_type=MESH)

    def arrive_a(src):
        return pltpu.make_async_remote_copy(
            src_ref=send_a.at[src], dst_ref=recv_a.at[src], send_sem=sa_sem.at[src], recv_sem=ra_sem.at[src],
            device_id=(px, src), device_id_type=MESH)

    def copy_b(s, part):
        to = lax.rem(px + s, PX)
        ks = pl.ds(part * KG, KG)
        return pltpu.make_async_remote_copy(
            src_ref=send_b.at[to, ks], dst_ref=recv_b.at[px, ks], send_sem=sb_sem.at[part, to],
            recv_sem=rb_sem.at[part, px], device_id=(to, py), device_id_type=MESH)

    def arrive_b(src, part):
        ks = pl.ds(part * KG, KG)
        return pltpu.make_async_remote_copy(
            src_ref=send_b.at[src, ks], dst_ref=recv_b.at[src, ks], send_sem=sb_sem.at[part, src],
            recv_sem=rb_sem.at[part, src], device_id=(src, py), device_id_type=MESH)

    def copy_m(to_x, h):
        return pltpu.make_async_remote_copy(
            src_ref=send_m.at[to_x, h], dst_ref=recv_m.at[py], send_sem=sm_sem.at[to_x, h], recv_sem=rm_sem.at[py],
            device_id=(to_x, 2 * px + h), device_id_type=MESH)

    def copy_n(to_y, r):
        return pltpu.make_async_remote_copy(
            src_ref=send_n.at[to_y, r], dst_ref=recv_n.at[px, py // 2], send_sem=sn_sem.at[to_y, r],
            recv_sem=rn_sem.at[px, py // 2], device_id=(4 * lax.rem(py, 2) + r, to_y), device_id_type=MESH)

    def own_n(to_y, r):
        return jnp.logical_and(4 * lax.rem(py, 2) + r == px, to_y == py)

    def arrive_n(src_x, t):
        return pltpu.make_async_remote_copy(
            src_ref=send_n.at[0, 0], dst_ref=recv_n.at[src_x, t], send_sem=sn_sem.at[0, 0],
            recv_sem=rn_sem.at[src_x, t], device_id=(src_x, 2 * t + px // 4), device_id_type=MESH)

    def copy_c(s):
        to = lax.rem(px + s, PX)
        return pltpu.make_async_remote_copy(
            src_ref=send_b.at[PX + to], dst_ref=recv_b.at[PX + px], send_sem=sc_sem.at[to], recv_sem=rc_sem.at[px],
            device_id=(to, py), device_id_type=MESH)

    def arrive_c(src):
        return pltpu.make_async_remote_copy(
            src_ref=send_b.at[PX + src], dst_ref=recv_b.at[PX + src], send_sem=sc_sem.at[src], recv_sem=rc_sem.at[src],
            device_id=(src, py), device_id_type=MESH)

    def copy_d(s, part):
        to = lax.rem(py + s, PY)
        ks = pl.ds(part * KG, KG)
        return pltpu.make_async_remote_copy(
            src_ref=send_a.at[PY + to, ks], dst_ref=lines_out.at[py, ks], send_sem=sd_sem.at[part, to],
            recv_sem=rd_sem.at[part, py], device_id=(px, to), device_id_type=MESH)

    def arrive_d(src, part):
        ks = pl.ds(part * KG, KG)
        return pltpu.make_async_remote_copy(
            src_ref=send_a.at[PY + src, ks], dst_ref=lines_out.at[src, ks], send_sem=sd_sem.at[part, src],
            recv_sem=rd_sem.at[part, src], device_id=(px, src), device_id_type=MESH)

    def z_forward(chunk):
        pltpu.make_async_copy(og.at[:, chunk], ogv.at[pl.ds(chunk * 4, 4)], og_sem.at[chunk]).wait()
        for jj in range(4):
            parts = []
            for j in (2 * jj, 2 * jj + 1):
                for b in range(4):
                    parts.append(ogv[chunk * 4 + b, pl.ds(j, 32, stride=8), :])
            rows = jnp.concatenate(parts, axis=0)
            high = rows.astype(BF)
            low = (rows - high.astype(F32)).astype(BF)
            both = dot_nt(zf[...], jnp.concatenate([high, low], axis=1))
            res = both[0:72] + both[72:144]
            blk[pl.ds(2 * jj, 72, stride=8), :] = res[:, 0:128]
            blk[pl.ds(2 * jj + 1, 72, stride=8), :] = res[:, 128:256]

    def step_a(s, c):
        to = lax.rem(py + s, PY)
        z_forward(to)
        send_a[to] = blk[0:528, :].reshape(KZ, 16, 128).astype(BF)

        @pl.when(s == 1)
        def _():
            pl.semaphore_wait(barrier, PX * PY - 1)

        copy_a(s).start()
        return c

    lax.fori_loop(1, PY, step_a, 0)
    z_forward(py)
    recv_a[py] = blk[0:528, :].reshape(KZ, 16, 128).astype(BF)

    def widen(k, c):
        rows = pl.ds(pl.multiple_of(k * 256, 256), 256)
        both = dot(xm[rows, :], dup[...])
        xr[rows, :] = both[:, 0:128]
        xi[rows, :] = both[:, 128:256]
        ogv[T1 + k] = jnp.zeros((256, 128), F32)
        ogv[T2 + k] = jnp.zeros((256, 128), F32)
        return c

    lax.fori_loop(0, 16, widen, 0)

    def wait_a(s, c):
        arrive_a(lax.rem(py + PY - s, PY)).wait_recv()
        return c

    lax.fori_loop(1, PY, wait_a, 0)

    def step_b(k, c):
        data = recv_a[0:PY, k].reshape(256, 128)
        both = dot(yf[...], data)
        res = (both[0:128] + both[128:256]).astype(BF)
        send_b[0:PX, k] = res.reshape(PX, 16, 128)
        return c

    def part_b(part, c):
        lax.fori_loop(part * KG, part * KG + KG, step_b, 0, unroll=True)

        def start_b(s, c2):
            copy_b(s, part).start()
            return c2

        return lax.fori_loop(1, PX, start_b, c)

    lax.fori_loop(0, 3, part_b, 0)
    pltpu.make_async_copy(xf_hbm, xfv, xf_sem).wait()

    def rows_c(data):
        data = data.astype(F32).reshape(KZ, 2, 8, 128)
        pad = jnp.zeros((8, 128), F32)
        parts = [jnp.concatenate([data[:, ri].reshape(264, 128), pad], axis=0).astype(BF) for ri in range(2)]
        lines[...] = jnp.concatenate(parts, axis=1)

    def term_c(src, cols):
        rows = pl.ds(pl.multiple_of(src * 256, 256), 256)
        return dot(lines[...], xfv[0, rows, cols]) + dot(lines[...], xfv[1, rows, cols])

    def arrive_c_rows(s):
        src = lax.rem(px + PX - s, PX)
        for part in range(3):
            arrive_b(src, part).wait_recv()
        rows_c(recv_b[src])
        return src

    rows_c(send_b[px])
    for k in range(4):
        sums[k] = term_c(px, slice(k * 256, k * 256 + 256))

    def step_gather(s, c):
        src = arrive_c_rows(s)
        for k in range(4):
            sums[k] = sums[k] + term_c(src, slice(k * 256, k * 256 + 256))
        return c

    lax.fori_loop(1, PX - 1, step_gather, 0)
    last_src = arrive_c_rows(PX - 1)

    def block_c(k):
        return lax.rem(px // 2 + py + k, 4)

    def step_c(k, c):
        pair = block_c(k)
        cols = pl.ds(pl.multiple_of(pair * 256, 256), 256)
        res = sums[pair] + term_c(last_src, cols)
        moved = dot(perm[...], res.astype(BF)).astype(BF)
        for e in range(2):
            send_m[2 * pair + e] = moved[:, e * 128:(e + 1) * 128].reshape(2, MR, 128)
        return c

    def chunks_c(k, act, act_own):
        for e in range(2):
            for h in range(2):
                to = 2 * block_c(k) + e
                own = jnp.logical_and(to == px, 2 * px + h == py)

                @pl.when(jnp.logical_not(own))
                def _():
                    act(to, h)

                @pl.when(own)
                def _():
                    act_own(to, h)

    def start_c(k, c):
        def own(to, h):
            local = pltpu.make_async_copy(send_m.at[to, h], recv_m.at[py], self_sem)
            local.start()
            local.wait()

        chunks_c(k, lambda to, h: copy_m(to, h).start(), own)
        return c

    def sent_c(k, c):
        chunks_c(k, lambda to, h: copy_m(to, h).wait_send(), lambda to, h: None)
        return c

    def first_c(k, c):
        step_c(k, c)
        return start_c(k, c)

    lax.fori_loop(0, 2, first_c, 0)
    lax.fori_loop(2, 4, step_c, 0)
    lax.fori_loop(0, 2, sent_c, 0)
    lax.fori_loop(2, 4, start_c, 0)

    def senders(k):
        first = lax.rem(px // 2 + 8 - owner_px // 2 - k, 4)
        return [first + 4 * m for m in range(4)]

    def place_modes(k):
        real, imag = [], []
        for src in senders(k):
            @pl.when(jnp.logical_not(jnp.logical_and(owner_px == px, src == py)))
            def _():
                pltpu.make_async_remote_copy(
                    src_ref=send_m.at[0, 0], dst_ref=recv_m.at[src], send_sem=sm_sem.at[0, 0], recv_sem=rm_sem.at[src],
                    device_id=(owner_px, src), device_id_type=MESH).wait_recv()

            turned = recv_m[src].astype(F32).T.astype(BF)
            real.append(turned[0:64])
            imag.append(turned[64:128])
        real, imag = jnp.concatenate(real, axis=0), jnp.concatenate(imag, axis=0)
        for r in range(4):
            cols = slice(r * 256, r * 256 + 256)
            res = dot(real, place[0, :, cols]) + dot(imag, place[1, :, cols])
            for m, src in enumerate(senders(k)):
                rows = pl.ds(r, 64, stride=4)
                ogv[G + src, rows, :] = res[m * 64:m * 64 + 64, 0:128]
                ogv[GS + src, rows, :] = res[m * 64:m * 64 + 64, 128:256]

    pltpu.make_async_copy(w_hbm, wv, w_sem).wait()

    def step_modes(pair, off, half):
        tv, uv = ogv.at[T1 + pair], ogv.at[T2 + pair]

        def add(k, acc):
            acc = list(acc)
            for src in senders(2 * half + k):
                gv, sv = ogv.at[G + src], ogv.at[GS + src]
                wp = [wv.at[2 * pair + ii, pl.ds(2 * src, 2)] for ii in range(2)]
                for oo in range(2):
                    w = [wp[ii][oo, off:off + 16, :].astype(F32) for ii in range(2)]
                    for b in range(4):
                        at = (b * 2 + oo) * 32 + off
                        gb = gv[at:at + 16, 0:66]
                        sb = sv[at:at + 16, 0:66]
                        for ii in range(2):
                            n = (ii * 4 + b) * 2
                            acc[n] = acc[n] + w[ii] * gb
                            acc[n + 1] = acc[n + 1] + w[ii] * sb
            return tuple(acc)

        places = [(ref, (b * 2 + ii) * 32 + off) for ii in range(2) for b in range(4) for ref in (tv, uv)]
        if half == 0:
            acc = tuple(jnp.zeros((16, 66), F32) for _ in places)
        else:
            acc = tuple(ref[at:at + 16, 0:66] for ref, at in places)
        acc = lax.fori_loop(0, 2, add, acc)
        for (ref, at), total in zip(places, acc):
            ref[at:at + 16, 0:66] = total

    def fold_modes(k):
        def rows_of(base, r):
            data = ogv[base + k, pl.ds(r, 64, stride=4), :]
            return data + pltpu.roll(data, 128 - KZ, 1)

        both = [jnp.concatenate([rows_of(T1, r), rows_of(T2, r)], axis=0).astype(BF) for r in range(4)]
        return dot_nt(back[...], jnp.concatenate(both, axis=0)).astype(BF)

    def send_modes(k):
        for e in range(4):
            r = lax.rem(px + e, 4)

            @pl.when(jnp.logical_not(own_n(k, r)))
            def _():
                copy_n(k, r).start()

            @pl.when(own_n(k, r))
            def _():
                local = pltpu.make_async_copy(send_n.at[k, r], recv_n.at[px, py // 2], self_sem)
                local.start()
                local.wait()

    def step_first(pair, c):
        step_modes(pair, 0, 0)
        step_modes(pair, 16, 0)
        return c

    def step_last(s, c):
        pairs = [lax.rem(py + 2 * s + e, PY) for e in range(2)]
        for pair in pairs:
            step_modes(pair, 0, 1)
            step_modes(pair, 16, 1)
        folded = [fold_modes(pair) for pair in pairs]
        for pair, chunk in zip(pairs, folded):
            for r in range(4):
                send_n[pair, r] = chunk[:, r * 128:(r + 1) * 128]
        for pair in pairs:
            send_modes(pair)
        return c

    place_modes(0)
    place_modes(1)
    lax.fori_loop(0, PY, step_first, 0)
    place_modes(2)
    place_modes(3)
    lax.fori_loop(0, PX, step_last, 0)

    def step_weight(i, c):
        for off in (0, 16):
            xrb = [xr[pl.ds(pl.multiple_of((b * 32 + i) * 32 + off, 16), 16), 0:66] for b in range(4)]
            xib = [xi[pl.ds(pl.multiple_of((b * 32 + i) * 32 + off, 16), 16), 0:66] for b in range(4)]

            def one(op, c2):
                gv, sv, out = ogv.at[G + op], ogv.at[GS + op], wv.at[i, pl.ds(2 * op, 2)]
                for oo in range(2):
                    total = None
                    for b in range(4):
                        at = (b * 2 + oo) * 32 + off
                        term = xrb[b] * gv[at:at + 16, 0:66] + xib[b] * sv[at:at + 16, 0:66]
                        total = term if total is None else total + term
                    out[oo, off:off + 16, :] = total.astype(BF)
                return c2

            lax.fori_loop(0, 16, one, 0)

        pltpu.make_async_copy(wv.at[i], wg.at[i], wg_sem.at[i]).start()
        return c

    lax.fori_loop(0, W1, step_weight, 0)

    def step_unplace(s, c):
        src = lax.rem(px + PX - s, PX)

        def wait_n(t, c2):
            @pl.when(jnp.logical_not(jnp.logical_and(src == px, 2 * t + px // 4 == py)))
            def _():
                arrive_n(src, t).wait_recv()

            return c2

        lax.fori_loop(0, 8, wait_n, 0)
        moved = dot(permt[...], recv_n[src].reshape(8 * NR, 128))
        dm[:, pl.ds(pl.multiple_of(src * 128, 128), 128)] = moved.astype(BF)
        return c

    lax.fori_loop(0, PX, step_unplace, 0)

    def x_inverse(to):
        rows = pl.ds(pl.multiple_of(to * 256, 256), 256)
        res = dot_nt(dm[...], xfv[0, rows, :]) + dot_nt(dm[...], xfv[1, rows, :])
        parts = [res[0:264, ri * 128:ri * 128 + 128].reshape(KZ, 8, 128) for ri in range(2)]
        return jnp.concatenate(parts, axis=1).astype(BF)

    def step_cb(s, c):
        to = lax.rem(px + s, PX)
        send_b[PX + to] = x_inverse(to)
        copy_c(s).start()
        return c

    lax.fori_loop(1, PX, step_cb, 0)
    recv_b[PX + px] = x_inverse(px)

    lax.fori_loop(W1, W2, step_weight, 0)

    def wait_c(s, c):
        arrive_c(lax.rem(px + PX - s, PX)).wait_recv()
        return c

    lax.fori_loop(1, PX, wait_c, 0)

    def step_bb(k, c):
        data = recv_b[PX:2 * PX, k].reshape(128, 128)
        res = dot(yi[...], jnp.concatenate([data, data], axis=0)).astype(BF)
        send_a[PY:2 * PY, k] = res.reshape(PY, 16, 128)
        return c

    def part_d(part, c):
        lax.fori_loop(part * KG, part * KG + KG, step_bb, 0, unroll=True)

        def start_d(s, c2):
            copy_d(s, part).start()
            return c2

        return lax.fori_loop(1, PY, start_d, c)

    lax.fori_loop(0, 3, part_d, 0)
    lax.fori_loop(W2, 32, step_weight, 0)

    own_lines = pltpu.make_async_copy(send_a.at[PY + py], lines_out.at[py], self_sem)
    own_lines.start()

    def step_d(s, c):
        for part in range(3):
            arrive_d(lax.rem(py + PY - s, PY), part).wait_recv()
        return c

    lax.fori_loop(1, PY, step_d, 0)
    own_lines.wait()

    def end_px(s, c):
        for part in range(3):
            copy_b(s, part).wait_send()
        copy_c(s).wait_send()
        return c

    def end_py(s, c):
        copy_a(s).wait_send()
        for part in range(3):
            copy_d(s, part).wait_send()
        return c

    def end_m(t, c):
        def end_n(r, c2):
            @pl.when(jnp.logical_not(own_n(t, r)))
            def _():
                copy_n(t, r).wait_send()

            return c2

        lax.fori_loop(0, 4, end_n, 0)
        return c

    def end_w(i, c):
        pltpu.make_async_copy(wv.at[i], wg.at[i], wg_sem.at[i]).wait()
        return c

    lax.fori_loop(1, PX, end_px, 0)
    lax.fori_loop(1, PY, end_py, 0)
    lax.fori_loop(2, 4, sent_c, 0)
    lax.fori_loop(0, PY, end_m, 0)
    lax.fori_loop(0, 32, end_w, 0)


def finish(held, lines, zi, wg, ig, buf, blk0, blk1, turn0, turn1, outv, in_sem, out_sem, ig_sem):
    def load(i):
        return pltpu.make_async_copy(held.at[pl.ds(2 * i, 2)], buf.at[pl.ds(2 * i, 2)], in_sem.at[i])

    def store(i):
        return pltpu.make_async_copy(buf.at[pl.ds(2 * i, 2)], wg.at[pl.ds(2 * i, 2)], out_sem.at[i])

    def start(i, c):
        load(i).start()
        return c

    lax.fori_loop(0, PY, start, 0)
    blk0[528:576, :] = jnp.zeros((48, 128), F32)
    blk1[528:576, :] = jnp.zeros((48, 128), F32)

    def step(k, c):
        slots = ((2 * k, blk0, turn0), (2 * k + 1, blk1, turn1))
        for src, blk, turn in slots:
            blk[0:528, :] = lines[src].astype(F32).reshape(528, 128)
        for j in range(8):
            for src, blk, turn in slots:
                turned = blk[pl.ds(j, 72, stride=8), :].T.astype(BF)
                turn[pl.ds(j, 128, stride=8), :] = dot(turned, zi[0]) + dot(turned, zi[1])
        for src, blk, turn in slots:
            outv[src] = turn[...].reshape(4, 256, 128).astype(BF)
        for src, blk, turn in slots:
            pltpu.make_async_copy(outv.at[src], ig.at[:, src], ig_sem.at[src]).start()

        @pl.when(k >= 3)
        def _():
            for e in range(2):
                load(2 * k - 6 + e).wait()
                store(2 * k - 6 + e).start()

        return c

    lax.fori_loop(0, PY // 2, step, 0)
    for i in range(10, 16):
        load(i).wait()
        store(i).start()

    def end(i, c):
        pltpu.make_async_copy(outv.at[i], ig.at[:, i], ig_sem.at[i]).wait()
        store(i).wait()
        return c

    lax.fori_loop(0, PY, end, 0)


def body(out_grad, input_modes, mode_weights):
    zf, zi, yf, yi, xf, perm, permt, place, back, dup = (jnp.asarray(t) for t in tables())
    og = out_grad.reshape(4, PY, 256, 128)
    xm = input_modes.reshape(4096, 66)
    w = mode_weights.reshape(32, 32, 32, 66)
    any_spec = pl.BlockSpec(memory_space=pl.ANY)
    vmem = pl.BlockSpec(memory_space=pltpu.VMEM)
    dma = pltpu.SemaphoreType.DMA
    held, lines = pl.pallas_call(
        kernel,
        out_shape=(
            jax.ShapeDtypeStruct((32, 32, 32, 66), BF),
            jax.ShapeDtypeStruct((PY, KZ, 16, 128), BF),
        ),
        in_specs=[any_spec, vmem, any_spec, any_spec] + [vmem] * 8,
        out_specs=(any_spec, any_spec),
        scratch_shapes=[
            pltpu.VMEM((4 * PY, 256, 128), F32),
            pltpu.VMEM((32, 32, 32, 66), BF),
            pltpu.VMEM((2, 2048, 1024), BF),
            pltpu.VMEM((2 * PY, KZ, 16, 128), BF),
            pltpu.VMEM((PY, KZ, 16, 128), BF),
            pltpu.VMEM((2 * PX, KZ, 16, 128), BF),
            pltpu.VMEM((2 * PX, KZ, 16, 128), BF),
            pltpu.VMEM((PX, 2, MR, 128), BF),
            pltpu.VMEM((PY, MR, 128), BF),
            pltpu.VMEM((PY, 4, NR, 128), BF),
            pltpu.VMEM((PX, 8, NR, 128), BF),
            pltpu.VMEM((CR, 256), BF),
            pltpu.VMEM((4, CR, 256), F32),
            pltpu.VMEM((CR, 1024), BF),
            pltpu.VMEM((4096, 128), F32),
            pltpu.VMEM((4096, 128), F32),
            pltpu.VMEM((576, 128), F32),
            dma((PY,)), dma, dma, dma((32,)), dma,
            dma((PY,)), dma((PY,)), dma((3, PX)), dma((3, PX)), dma((PX, 2)), dma((PY,)),
            dma((PY, 4)), dma((PX, 8)), dma((PX,)), dma((PX,)), dma((3, PY)), dma((3, PY)),
        ],
        compiler_params=pltpu.CompilerParams(
            collective_id=0, has_side_effects=True, vmem_limit_bytes=54 * 1024 * 1024
        ),
    )(og, xm, w, xf, zf, yf, yi, perm, permt, place, back, dup)
    wg, ig = pl.pallas_call(
        finish,
        out_shape=(
            jax.ShapeDtypeStruct((32, 32, 32, 66), BF),
            jax.ShapeDtypeStruct((4, PY, 256, 128), BF),
        ),
        in_specs=[any_spec, vmem, vmem],
        out_specs=(any_spec, any_spec),
        scratch_shapes=[
            pltpu.VMEM((32, 32, 32, 66), BF),
            pltpu.VMEM((576, 128), F32),
            pltpu.VMEM((576, 128), F32),
            pltpu.VMEM((1024, 128), F32),
            pltpu.VMEM((1024, 128), F32),
            pltpu.VMEM((PY, 4, 256, 128), BF),
            dma((PY,)), dma((PY,)), dma((PY,)),
        ],
        compiler_params=pltpu.CompilerParams(vmem_limit_bytes=54 * 1024 * 1024),
        cost_estimate=pl.CostEstimate(flops=600000000, bytes_accessed=23000000, transcendentals=0),
    )(held, lines, zi)
    return wg.reshape(32, 32, 8, 4, 66), ig.reshape(4, 32, 16, 8, 128)


def solution(mesh):
    spec = P(None, None, "px", "py", None)
    return jax.shard_map(
        body, mesh=mesh, in_specs=(spec, spec, spec), out_specs=(spec, spec), check_vma=False
    )
```

time: 157 us -> 149 us (0.949); the launches traced: 154 us -> 149 us
  Pallas kernels: 151 us -> 148 us
  local copies, waits for them, and re-layouts: 2.85 us -> 0 us
    pallas_call x1, Pallas kernels: 144 us -> 139 us  [body(): pl.pallas_call(kernel, out_shape=(jax.ShapeDtypeStruct((32, 32, 32, 66),...]
    pallas_call x1, Pallas kernels: 6.72 us -> 9.64 us  [body(): pl.pallas_call(finish, out_shape=(jax.ShapeDtypeStruct((32, 32, 32, 66),...]
    unnamed x3 -> x0, local copies, waits for them, and re-layouts: 2.85 us -> none
where the time goes in v3:
time: 149 us
  Pallas kernels  148 us (99%)
    pallas_call x1, Pallas kernels, body(): pl.pallas_call(kernel, out_shape=(jax.ShapeDtypeStruct((32, 32, 32, 66),...  139 us
    pallas_call x1, Pallas kernels, body(): pl.pallas_call(finish, out_shape=(jax.ShapeDtypeStruct((32, 32, 32, 66),...  9.64 us

profile of v3, /device:TPU:9, one launch (start us, length us, event | category | flops | bytes accessed | tf_op | source)
XLA Modules:
  0.0 148.9 jit_solution(14595548974826909305)
XLA Ops:
  0.6 138.6 %shard_map.140 = (bf16[32,32,32,66]{3,2,1,0:T(8,128)(2,1)}, bf16[16,33,16,128]{3,2,1,0:T(8,128)(2,1)}) custom-call(f32[4,16,256,128]{3,2,1,0:T(8,128)} %bitcast.5, bf16[4096,66]{1,0:T(8,128)(2,1)} %bitcast.7, bf16[32,32,32,66]{3,2,1,0:T(8,128)(2,1)} %bitcast.6, bf16[2,2048,1024]{2,1,0:T(8,128)(2,1)} %constant.24.clone.xf_hbm, ...), custom_call_target="tpu_custom_call" | custom-call | tf_op jit(solution)/shard_map/pallas_call | solution.py:645
  139.3 9.6 %shard_map.141 = (bf16[32,32,32,66]{3,2,1,0:T(8,128)(2,1)}, bf16[4,16,256,128]{3,2,1,0:T(8,128)(2,1)}) custom-call(bf16[32,32,32,66]{3,2,1,0:T(8,128)(2,1)} %get-tuple-element.6.held, bf16[16,33,16,128]{3,2,1,0:T(8,128)(2,1)} %get-tuple-element.7.lines, bf16[2,72,128]{2,1,0:T(8,128)(2,1)} %constant.21.clone.zi), custom_call_target="tpu_custom_call" | custom-call | flops 600000000 | bytes 23000000 | tf_op jit(solution)/shard_map/pallas_call | solution.py:679

commit v4 on v3

--- a/solution.py
+++ b/solution.py
@@ -18,7 +18,8 @@
 PX = 8
 PY = 16
 MR = 144
-W1, W2 = 7, 20
+AHEAD = 4
+W1, W2 = 5, 18
 KG = 11
 NR = 48
 CR = 272
@@ -129,11 +130,12 @@
     py = lax.axis_index("py")
     owner_px = py // 2
 
-    for k in range(PY):
-        chunk = lax.rem(py + 1 + k, PY)
+    def load_og(s):
+        chunk = lax.rem(py + s, PY)
         pltpu.make_async_copy(og.at[:, chunk], ogv.at[pl.ds(chunk * 4, 4)], og_sem.at[chunk]).start()
-    pltpu.make_async_copy(xf_hbm, xfv, xf_sem).start()
-    pltpu.make_async_copy(w_hbm, wv, w_sem).start()
+
+    for s in range(1, AHEAD + 1):
+        load_og(s)
 
     barrier = pltpu.get_barrier_semaphore()
     me = px * PY + py
@@ -228,6 +230,11 @@
 
     def step_a(s, c):
         to = lax.rem(py + s, PY)
+
+        @pl.when(s <= PY - AHEAD)
+        def _():
+            load_og(s + AHEAD)
+
         z_forward(to)
         send_a[to] = blk[0:528, :].reshape(KZ, 16, 128).astype(BF)
 
@@ -239,6 +246,8 @@
         return c
 
     lax.fori_loop(1, PY, step_a, 0)
+    pltpu.make_async_copy(xf_hbm, xfv, xf_sem).start()
+    pltpu.make_async_copy(w_hbm, wv, w_sem).start()
     z_forward(py)
     recv_a[py] = blk[0:528, :].reshape(KZ, 16, 128).astype(BF)
 
@@ -493,11 +502,12 @@
             return c2
 
         lax.fori_loop(0, 8, wait_n, 0)
-        moved = dot(permt[...], recv_n[src].reshape(8 * NR, 128))
-        dm[:, pl.ds(pl.multiple_of(src * 128, 128), 128)] = moved.astype(BF)
         return c
 
     lax.fori_loop(0, PX, step_unplace, 0)
+    for k in range(4):
+        data = jnp.concatenate([recv_n[2 * k + e].reshape(8 * NR, 128) for e in range(2)], axis=1)
+        dm[:, k * 256:k * 256 + 256] = dot(permt[...], data).astype(BF)
 
     def x_inverse(to):
         rows = pl.ds(pl.multiple_of(to * 256, 256), 256)

time: 149 us -> 148 us (level)
    pallas_call x1, Pallas kernels: 139 us -> 137 us  [body(): pl.pallas_call(kernel, out_shape=(jax.ShapeDtypeStruct((32, 32, 32, 66),...]
where the time goes in v4:
time: 148 us; the launch traced here: 147 us
  Pallas kernels  147 us (99%)
    pallas_call x1, Pallas kernels, body(): pl.pallas_call(kernel, out_shape=(jax.ShapeDtypeStruct((32, 32, 32, 66),...  137 us
    pallas_call x1, Pallas kernels, body(): pl.pallas_call(finish, out_shape=(jax.ShapeDtypeStruct((32, 32, 32, 66),...  9.64 us

profile of v4, /device:TPU:9, one launch (start us, length us, event | category | flops | bytes accessed | tf_op | source)
XLA Modules:
  0.0 147.3 jit_solution(15240991375244674928)
XLA Ops:
  0.6 137.0 %shard_map.140 = (bf16[32,32,32,66]{3,2,1,0:T(8,128)(2,1)}, bf16[16,33,16,128]{3,2,1,0:T(8,128)(2,1)}) custom-call(f32[4,16,256,128]{3,2,1,0:T(8,128)} %bitcast.5, bf16[4096,66]{1,0:T(8,128)(2,1)} %bitcast.7, bf16[32,32,32,66]{3,2,1,0:T(8,128)(2,1)} %bitcast.6, bf16[2,2048,1024]{2,1,0:T(8,128)(2,1)} %constant.24.clone.xf_hbm, ...), custom_call_target="tpu_custom_call" | custom-call | tf_op jit(solution)/shard_map/pallas_call | solution.py:655
  137.7 9.6 %shard_map.141 = (bf16[32,32,32,66]{3,2,1,0:T(8,128)(2,1)}, bf16[4,16,256,128]{3,2,1,0:T(8,128)(2,1)}) custom-call(bf16[32,32,32,66]{3,2,1,0:T(8,128)(2,1)} %get-tuple-element.6.held, bf16[16,33,16,128]{3,2,1,0:T(8,128)(2,1)} %get-tuple-element.7.lines, bf16[2,72,128]{2,1,0:T(8,128)(2,1)} %constant.21.clone.zi), custom_call_target="tpu_custom_call" | custom-call | flops 600000000 | bytes 23000000 | tf_op jit(solution)/shard_map/pallas_call | solution.py:689

commit v5 on v4

--- a/solution.py
+++ b/solution.py
@@ -623,18 +623,15 @@
         for src, blk, turn in slots:
             pltpu.make_async_copy(outv.at[src], ig.at[:, src], ig_sem.at[src]).start()
 
-        @pl.when(k >= 3)
+        @pl.when(jnp.logical_and(k >= 3, k < 7))
         def _():
-            for e in range(2):
-                load(2 * k - 6 + e).wait()
-                store(2 * k - 6 + e).start()
+            for e in range(4):
+                load(4 * k - 12 + e).wait()
+                store(4 * k - 12 + e).start()
 
         return c
 
     lax.fori_loop(0, PY // 2, step, 0)
-    for i in range(10, 16):
-        load(i).wait()
-        store(i).start()
 
     def end(i, c):
         pltpu.make_async_copy(outv.at[i], ig.at[:, i], ig_sem.at[i]).wait()

time: 148 us -> 148 us (level)
  no operation moved by 1% of the time
where the time goes in v5:
time: 148 us; the launch traced here: 147 us
  Pallas kernels  146 us (99%)
    pallas_call x1, Pallas kernels, body(): pl.pallas_call(kernel, out_shape=(jax.ShapeDtypeStruct((32, 32, 32, 66),...  137 us
    pallas_call x1, Pallas kernels, body(): pl.pallas_call(finish, out_shape=(jax.ShapeDtypeStruct((32, 32, 32, 66),...  8.84 us

profile of v5, /device:TPU:9, one launch (start us, length us, event | category | flops | bytes accessed | tf_op | source)
XLA Modules:
  0.0 146.5 jit_solution(3827216062296575360)
XLA Ops:
  0.6 137.0 %shard_map.140 = (bf16[32,32,32,66]{3,2,1,0:T(8,128)(2,1)}, bf16[16,33,16,128]{3,2,1,0:T(8,128)(2,1)}) custom-call(f32[4,16,256,128]{3,2,1,0:T(8,128)} %bitcast.5, bf16[4096,66]{1,0:T(8,128)(2,1)} %bitcast.7, bf16[32,32,32,66]{3,2,1,0:T(8,128)(2,1)} %bitcast.6, bf16[2,2048,1024]{2,1,0:T(8,128)(2,1)} %constant.24.clone.xf_hbm, ...), custom_call_target="tpu_custom_call" | custom-call | tf_op jit(solution)/shard_map/pallas_call | solution.py:652
  137.7 8.8 %shard_map.141 = (bf16[32,32,32,66]{3,2,1,0:T(8,128)(2,1)}, bf16[4,16,256,128]{3,2,1,0:T(8,128)(2,1)}) custom-call(bf16[32,32,32,66]{3,2,1,0:T(8,128)(2,1)} %get-tuple-element.6.held, bf16[16,33,16,128]{3,2,1,0:T(8,128)(2,1)} %get-tuple-element.7.lines, bf16[2,72,128]{2,1,0:T(8,128)(2,1)} %constant.21.clone.zi), custom_call_target="tpu_custom_call" | custom-call | flops 600000000 | bytes 23000000 | tf_op jit(solution)/shard_map/pallas_call | solution.py:686
